TPU v7x, 32 devices: a whole 2x2x4 slice. The times are simulated.
32 devices in a mesh: dp: 8 (over z, x), mp: 4 (over y, core).
Axes of the slice: x: 2, y: 2, z: 4, core: 2. Of those that a mesh axis runs over, the one named last changes fastest.
Arguments:
- tokens: bfloat16 [16384, 896], P(('dp', 'mp')), may hold values from -6 to 6
- seq_lengths: int32 [8, 3], P('dp'), may hold values from 1 to 1536, as said below
- attn_gain: bfloat16 [896], replicated, may hold values from 0.5 to 1.5
- qkv_weight: bfloat16 [896, 1152], replicated, may hold values from -0.1875 to 0.1875
- qkv_bias: bfloat16 [1152], replicated, may hold values from -3 to 3
- out_weight: bfloat16 [896, 896], replicated, may hold values from -3.5 to 3.5
- mlp_gain: bfloat16 [896], replicated, may hold values from 0.5 to 1.5
- gate_weight: bfloat16 [896, 4864], P(None, 'mp'), may hold values from -0.1875 to 0.1875
- up_weight: bfloat16 [896, 4864], P(None, 'mp'), may hold values from -0.1875 to 0.1875
- down_weight: bfloat16 [4864, 896], P('mp'), may hold values from -0.078125 to 0.078125
- cotangent: bfloat16 [16384, 896], P(('dp', 'mp')), may hold values from -6 to 6
Outputs:
- output: bfloat16 [16384, 896], P(('dp', 'mp'))
- grad_tokens: float32 [16384, 896], P(('dp', 'mp'))
- grad_attn_gain: float32 [896], replicated
- grad_qkv_weight: float32 [896, 1152], replicated
- grad_qkv_bias: float32 [1152], replicated
- grad_out_weight: float32 [896, 896], replicated
- grad_mlp_gain: float32 [896], replicated
- grad_gate: float32 [896, 4864], P('dp', 'mp')
- grad_up: float32 [896, 4864], P('dp', 'mp')
- grad_down: float32 [4864, 896], P('mp', 'dp')
Inputs may be any that keep to these rules, and one draw needn't show every extreme that they name: `seq_lengths`: each row sums to 2048; its middle entry is 1536; its first and last entries are positive and sum to 512; in some row the first entry is 1.
All inputs are finite; a program needn't handle non-finite values.
Results may differ from a plain program's by a relative error of at most 0.011.
Values may be sent and summed in bfloat16 or wider, within the bound.
No kernel may reach another device: no remote copies, remote signals or barrier semaphores. Data moves between devices by JAX's collectives and lax.ppermute only.
A program may use at most 256 MiB of HBM per device.

v0:
```python
import jax
import jax.numpy as jnp
from jax import lax
from jax.sharding import PartitionSpec as P

HEADS = 14
KV_HEADS = 2
HEAD = 64


norm_epsilon = 1e-06
rope_base = 1000000.0
masked_score = -1e30


def rope_tables(position, head_size):
    half_size = head_size // 2
    inverse_freq = rope_base ** (-2.0 * jnp.arange(half_size, dtype=jnp.float32) / head_size)
    angles = position.astype(jnp.float32)[:, None] * inverse_freq[None, :]
    return (jnp.cos(angles)[:, None, :], jnp.sin(angles)[:, None, :])


def rotate(values, cos_table, sin_table):
    half_size = values.shape[-1] // 2
    lower_half = values[..., :half_size]
    upper_half = values[..., half_size:]
    return jnp.concatenate(
        [
            lower_half * cos_table - upper_half * sin_table,
            upper_half * cos_table + lower_half * sin_table,
        ],
        axis=-1,
    )


def layout(length_row, positions):
    seq_ends = jnp.cumsum(length_row)
    segment = jnp.sum((positions[:, None] >= seq_ends[None, :]).astype(jnp.int32), axis=1)
    starts = seq_ends - length_row
    slot_ids = jnp.arange(length_row.shape[0], dtype=jnp.int32)
    seq_begin = jnp.sum(
        jnp.where(segment[:, None] == slot_ids[None, :], starts[None, :], 0), axis=1
    )
    return (segment, positions - seq_begin)


def rms_apply(values, gain_vec):
    inverse = lax.rsqrt(jnp.mean(values * values, axis=-1, keepdims=True) + norm_epsilon)
    return (values * inverse * gain_vec, inverse)


def rms_back(values, inverse, gain_vec, grad_out):
    scaled = grad_out * gain_vec
    mean_dot = jnp.mean(values * scaled, axis=-1, keepdims=True)
    grad_in = inverse * scaled - values * inverse * inverse * inverse * mean_dot
    grad_gain = jnp.sum(grad_out * values * inverse, axis=0)
    return (grad_in, grad_gain)


def row_contract(left_mat, right_mat):
    return lax.dot_general(
        left_mat, right_mat, (((0,), (0,)), ((), ())), preferred_element_type=jnp.float32
    )


def col_contract(left_mat, right_mat):
    return lax.dot_general(
        left_mat, right_mat, (((1,), (1,)), ((), ())), preferred_element_type=jnp.float32
    )


def gated_back(gate_act, up_act, grad_hidden):
    sigmoid_gate = jax.nn.sigmoid(gate_act)
    grad_gate_act = (
        grad_hidden * up_act * sigmoid_gate * (1.0 + gate_act * (1.0 - sigmoid_gate))
    ).astype(jnp.bfloat16)
    grad_up_act = (grad_hidden * gate_act * sigmoid_gate).astype(jnp.bfloat16)
    return (grad_gate_act, grad_up_act)


def attend_head(head_parts, allowed, score_scale):
    query_head, key_head, value_head = head_parts
    scores = jnp.where(allowed, col_contract(query_head, key_head) * score_scale, masked_score)
    row_max = jnp.max(scores, axis=1, keepdims=True)
    weights = jnp.exp(scores - row_max)
    summed = jnp.sum(weights, axis=1, keepdims=True)
    attn_prob = (weights / summed).astype(jnp.bfloat16)
    head_out = jnp.dot(attn_prob, value_head, preferred_element_type=jnp.float32).astype(
        jnp.bfloat16
    )
    return (head_out, (row_max + jnp.log(summed))[:, 0])


def attend_back(head_parts, allowed, score_scale):
    query_head, key_head, value_head, grad_head, log_total = head_parts
    scores = jnp.where(allowed, col_contract(query_head, key_head) * score_scale, masked_score)
    attn_prob = jnp.exp(scores - log_total[:, None])
    grad_prob = col_contract(grad_head, value_head)
    row_dot = jnp.sum(attn_prob * grad_prob, axis=1, keepdims=True)
    grad_score = (attn_prob * (grad_prob - row_dot)).astype(jnp.bfloat16)
    grad_query = jnp.dot(grad_score, key_head, preferred_element_type=jnp.float32) * score_scale
    grad_key = row_contract(grad_score, query_head) * score_scale
    grad_value = row_contract(attn_prob.astype(jnp.bfloat16), grad_head)
    return (grad_query, grad_key, grad_value)


def on_device(
    tokens,
    seq_lengths,
    attn_gain,
    qkv_weight,
    qkv_bias,
    out_weight,
    mlp_gain,
    gate_weight,
    up_weight,
    down_weight,
    cotangent,
):
    tok_rows = tokens.shape[0]
    mp_count = lax.axis_size("mp")
    mp_index = lax.axis_index("mp")
    group_rows = tok_rows * mp_count
    longest = group_rows - tok_rows
    window = longest + tok_rows
    q_width = HEADS * HEAD
    kv_width = KV_HEADS * HEAD
    repeat_count = HEADS // KV_HEADS
    score_scale = HEAD ** (-0.5)
    row_base = mp_index * tok_rows
    own_rows = row_base + jnp.arange(tok_rows, dtype=jnp.int32)
    key_rows = row_base - longest + jnp.arange(window, dtype=jnp.int32)
    segment, position = layout(seq_lengths[0], own_rows)
    key_segment, key_position = layout(seq_lengths[0], key_rows)
    key_segment = jnp.where(key_rows >= 0, key_segment, -1)
    allowed = (segment[:, None] == key_segment[None, :]) & (own_rows[:, None] >= key_rows[None, :])
    cos_table, sin_table = rope_tables(position, HEAD)
    inputs = tokens.astype(jnp.float32)
    attn_scale = attn_gain.astype(jnp.float32)
    normed_full, inverse_one = rms_apply(inputs, attn_scale)
    normed = normed_full.astype(jnp.bfloat16)
    projected = jnp.dot(normed, qkv_weight, preferred_element_type=jnp.float32) + qkv_bias.astype(
        jnp.float32
    )
    queries = rotate(
        projected[:, :q_width].reshape(tok_rows, HEADS, HEAD), cos_table, sin_table
    ).astype(jnp.bfloat16)
    keys_own = (
        rotate(
            projected[:, q_width : q_width + kv_width].reshape(tok_rows, KV_HEADS, HEAD),
            cos_table,
            sin_table,
        )
        .astype(jnp.bfloat16)
        .reshape(tok_rows, kv_width)
    )
    values_own = projected[:, q_width + kv_width :].astype(jnp.bfloat16)
    keys_group, values_group = (
        lax.all_gather(keys_own, "mp", axis=0, tiled=True),
        lax.all_gather(values_own, "mp", axis=0, tiled=True),
    )
    padding = jnp.zeros((longest, kv_width), jnp.bfloat16)
    win_keys = lax.dynamic_slice_in_dim(
        jnp.concatenate([padding, keys_group], axis=0), row_base, window, 0
    )
    win_values = lax.dynamic_slice_in_dim(
        jnp.concatenate([padding, values_group], axis=0), row_base, window, 0
    )
    key_heads = jnp.repeat(
        win_keys.reshape(window, KV_HEADS, HEAD).transpose(1, 0, 2), repeat_count, axis=0
    )
    value_heads = jnp.repeat(
        win_values.reshape(window, KV_HEADS, HEAD).transpose(1, 0, 2), repeat_count, axis=0
    )
    query_heads = queries.transpose(1, 0, 2)
    attended_heads, log_totals = lax.map(
        lambda head_parts: attend_head(head_parts, allowed, score_scale),
        (query_heads, key_heads, value_heads),
    )
    attended = attended_heads.transpose(1, 0, 2).reshape(tok_rows, q_width)
    middle = inputs + jnp.dot(attended, out_weight, preferred_element_type=jnp.float32)
    mlp_scale = mlp_gain.astype(jnp.float32)
    normed_mid_full, inverse_two = rms_apply(middle, mlp_scale)
    normed_mid = normed_mid_full.astype(jnp.bfloat16)
    gathered = lax.all_gather(normed_mid, "mp", axis=0, tiled=True)
    gate_act = jnp.dot(gathered, gate_weight, preferred_element_type=jnp.float32)
    up_act = jnp.dot(gathered, up_weight, preferred_element_type=jnp.float32)
    hidden = (jax.nn.silu(gate_act) * up_act).astype(jnp.bfloat16)
    mlp_out = lax.psum_scatter(
        jnp.dot(hidden, down_weight, preferred_element_type=jnp.float32).astype(jnp.bfloat16),
        "mp",
        scatter_dimension=0,
        tiled=True,
    ).astype(jnp.float32)
    output = (middle + mlp_out).astype(jnp.bfloat16)
    grad_rows = lax.all_gather(cotangent, "mp", axis=0, tiled=True)
    grad_down = row_contract(hidden, grad_rows)
    grad_hidden = col_contract(grad_rows, down_weight)
    grad_gate_act, grad_up_act = gated_back(gate_act, up_act, grad_hidden)
    grad_gate = row_contract(gathered, grad_gate_act)
    grad_up = row_contract(gathered, grad_up_act)
    grad_normed_mid = lax.psum_scatter(
        col_contract(grad_gate_act, gate_weight) + col_contract(grad_up_act, up_weight),
        "mp",
        scatter_dimension=0,
        tiled=True,
    )
    grad_gate, grad_up, grad_down = (
        lax.psum_scatter(grad_gate, "dp", scatter_dimension=0, tiled=True),
        lax.psum_scatter(grad_up, "dp", scatter_dimension=0, tiled=True),
        lax.psum_scatter(grad_down, "dp", scatter_dimension=1, tiled=True),
    )
    grad_from_mid, grad_mlp_gain = rms_back(middle, inverse_two, mlp_scale, grad_normed_mid)
    grad_middle = cotangent.astype(jnp.float32) + grad_from_mid
    grad_branch = grad_middle.astype(jnp.bfloat16)
    grad_out_weight = row_contract(attended, grad_branch)
    grad_attended = col_contract(grad_branch, out_weight).astype(jnp.bfloat16)
    grad_heads = grad_attended.reshape(tok_rows, HEADS, HEAD).transpose(1, 0, 2)
    grad_query_heads, grad_key_heads, grad_value_heads = lax.map(
        lambda head_parts: attend_back(head_parts, allowed, score_scale),
        (query_heads, key_heads, value_heads, grad_heads, log_totals),
    )
    grad_win_keys = grad_key_heads.reshape(KV_HEADS, repeat_count, window, HEAD).sum(axis=1)
    grad_win_keys = grad_win_keys.transpose(1, 0, 2).reshape(window, kv_width)
    grad_win_values = grad_value_heads.reshape(KV_HEADS, repeat_count, window, HEAD).sum(axis=1)
    grad_win_values = grad_win_values.transpose(1, 0, 2).reshape(window, kv_width)
    zeros_group = jnp.zeros((longest + group_rows, kv_width), jnp.float32)
    key_spread = lax.dynamic_update_slice_in_dim(zeros_group, grad_win_keys, row_base, 0)[longest:]
    value_spread = lax.dynamic_update_slice_in_dim(zeros_group, grad_win_values, row_base, 0)[
        longest:
    ]
    grad_keys_own, grad_values_own = (
        lax.psum_scatter(key_spread, "mp", scatter_dimension=0, tiled=True),
        lax.psum_scatter(value_spread, "mp", scatter_dimension=0, tiled=True),
    )
    grad_query = rotate(grad_query_heads.transpose(1, 0, 2), cos_table, -sin_table)
    grad_query = grad_query.astype(jnp.bfloat16).reshape(tok_rows, q_width)
    grad_key = rotate(grad_keys_own.reshape(tok_rows, KV_HEADS, HEAD), cos_table, -sin_table)
    grad_key = grad_key.astype(jnp.bfloat16).reshape(tok_rows, kv_width)
    grad_value = grad_values_own.astype(jnp.bfloat16)
    grad_projected = jnp.concatenate([grad_query, grad_key, grad_value], axis=1)
    grad_qkv_weight = row_contract(normed, grad_projected)
    grad_qkv_bias = jnp.sum(grad_projected.astype(jnp.float32), axis=0)
    grad_normed = col_contract(grad_projected, qkv_weight)
    grad_from_first, grad_attn_gain = rms_back(inputs, inverse_one, attn_scale, grad_normed)
    grad_tokens = grad_middle + grad_from_first
    summed_grads = lax.psum(
        (grad_attn_gain, grad_qkv_weight, grad_qkv_bias, grad_out_weight, grad_mlp_gain),
        ("dp", "mp"),
    )
    return (
        output,
        grad_tokens,
        summed_grads[0],
        summed_grads[1],
        summed_grads[2],
        summed_grads[3],
        summed_grads[4],
        grad_gate,
        grad_up,
        grad_down,
    )


def solution(mesh):
    return jax.shard_map(
        on_device,
        mesh=mesh,
        in_specs=(
            P(("dp", "mp"), None),
            P("dp", None),
            P(),
            P(),
            P(),
            P(),
            P(),
            P(None, "mp"),
            P(None, "mp"),
            P("mp", None),
            P(("dp", "mp"), None),
        ),
        out_specs=(
            P(("dp", "mp"), None),
            P(("dp", "mp"), None),
            P(),
            P(),
            P(),
            P(),
            P(),
            P("dp", "mp"),
            P("dp", "mp"),
            P("mp", "dp"),
        ),
        check_vma=False,
    )
```

profile of v0, /device:TPU:0, one launch (start us, length us, event | category | flops | bytes accessed | tf_op | source)
XLA Modules:
  0.0 1102.3 jit_solution(3638521645501212788)
XLA Ops:
  10.2 3.4 convolution_add_fusion.1
  16.6 8.6 all_gather.12
  27.7 2.7 copy.40
  35.7 7.3 all_gather.13
  49.1 4.3 broadcast_in_dim.94
  53.4 4.3 broadcast_in_dim.96
  57.7 125.8 %while.28 = (s32[]{:T(128)}, bf16[14,512,64]{1,2,0:T(8,128)(2,1)}, f32[14,512]{1,0:T(8,128)S(1)}, bf16[14,512,64]{2,1,0:T(8,128)(2,1)}, bf16[14,2048,64]{2,1,0:T...) while((s32[]{:T(128)}, bf16[14,512,64]{1,2,0:T(8,128)(2,1)}, ...), condition=%wide.region_8.9_spmd.clone, body=%wide.region_5.8_spmd.clone.sunk | while | flops 280002048 | bytes 30648468 | solution.py:176
  62.8 3.9 fusion.115
  71.8 3.9 fusion.115
  80.8 3.9 fusion.115
  89.7 3.9 fusion.115
  98.7 3.9 fusion.115
  107.7 3.9 fusion.115
  116.7 3.9 fusion.115
  125.7 3.9 fusion.115
  134.6 3.9 fusion.115
  143.6 3.9 fusion.115
  152.6 3.9 fusion.115
  161.6 3.9 fusion.115
  170.6 3.9 fusion.115
  179.5 3.9 fusion.115
  183.5 3.1 multiply_reduce_fusion.3
  190.2 31.3 %all-gather.3.cloned.1.call-done = bf16[2048,896]{1,0:T(8,128)(2,1)} async-done(((bf16[512,896]{1,0:T(8,128)(2,1)}), bf16[2048,896]{1,0:T(8,128)(2,1)}) %all-gather.3.cloned.1.call-update) | async-done | bytes 3670032 | tf_op jit(solution)/shard_map/all_gather | solution.py:185
  221.5 10.5 fusion.64
  232.0 7.8 fusion.65
  239.8 14.8 %all-gather.5.cloned.1.call-done = bf16[2048,896]{1,0:T(8,128)(2,1)} async-done(((bf16[512,896]{1,0:T(8,128)(2,1)}), bf16[2048,896]{1,0:T(8,128)(2,1)}) %all-gather.5.cloned.1.call-update) | async-done | bytes 3670032 | tf_op jit(solution)/shard_map/all_gather | solution.py:196
  254.6 18.9 %multiply_convert_fusion.1 = (bf16[2048,1216]{0,1:T(8,128)(2,1)}, bf16[2048,1216]{0,1:T(8,128)(2,1)}, bf16[2048,1216]{0,1:T(8,128)(2,1)}) fusion(f32[2048,1216]{0,1:T(8,128)} %fusion.64, f32[2048,1216]{0,1:T(8,128)} %fusion.65, bf16[2048,896]{1,0:T(8,128)(2,1)} %all-gather.5.cloned.1.call-done, bf16[1216,896]{1,0:T(8,128)(2,1)S(1)} %copy-done), kind=kOutput, calls=%fused_computation.52 | convolution fusion | flops 4502585344 | bytes 40714240 | tf_op jit(solution)/shard_map/dot_general | solution.py:67
  273.5 7.9 fusion.66
  281.4 8.1 convolution_add_fusion
  289.7 9.5 convolution_convert_fusion
  299.3 55.8 %reduce-scatter.10.cloned.1.call-done = f32[512,896]{1,0:T(8,128)} async-done(((f32[2048,896]{1,0:T(8,128)}), f32[512,896]{1,0:T(8,128)}) %reduce-scatter.10.cloned.1.call-update) | async-done | bytes 1835024 | tf_op jit(solution)/shard_map/reduce_scatter | solution.py:202
  357.1 42.4 %reduce-scatter.8.cloned.1.call-done = bf16[512,896]{1,0:T(8,128)(2,1)} async-done(((bf16[2048,896]{1,0:T(8,128)(2,1)}), bf16[512,896]{1,0:T(8,128)(2,1)}) %reduce-scatter.8.cloned.1.call-update) | async-done | bytes 917520 | tf_op jit(solution)/shard_map/reduce_scatter | solution.py:189
  399.5 4.0 subtract_add_fusion
  407.2 156.2 %while.29 = (s32[]{:T(128)}, f32[14,512,64]{1,2,0:T(8,128)}, f32[14,2048,64]{1,2,0:T(8,128)}, f32[14,2048,64]{1,2,0:T(8,128)}, bf16[14,512,64]{2,1,0:T(8,128)(2,...) while((s32[]{:T(128)}, f32[14,512,64]{1,2,0:T(8,128)}, ...), condition=%wide.region_15.16_spmd.clone, body=%wide.region_13.15_spmd.clone.sunk | while | flops 683834880 | bytes 34638984 | solution.py:219
  409.0 2.9 multiply_reduce_fusion.5
  420.2 2.9 multiply_reduce_fusion.5
  431.4 2.9 multiply_reduce_fusion.5
  442.5 2.9 multiply_reduce_fusion.5
  453.6 2.9 multiply_reduce_fusion.5
  464.8 2.9 multiply_reduce_fusion.5
  476.0 2.9 multiply_reduce_fusion.5
  487.1 2.9 multiply_reduce_fusion.5
  498.3 2.9 multiply_reduce_fusion.5
  509.4 2.9 multiply_reduce_fusion.5
  520.6 2.9 multiply_reduce_fusion.5
  531.8 2.9 multiply_reduce_fusion.5
  542.9 2.9 multiply_reduce_fusion.5
  554.0 2.9 multiply_reduce_fusion.5
  563.3 3.9 reduce_sum.133
  568.6 3.9 reduce_sum.132
  574.1 10.9 fusion.67
  585.1 10.6 fusion.68
  596.1 10.7 fusion.69
  610.6 2.8 fusion.54
  614.4 7.3 reduce-scatter.12.cloned.1.call-done
  622.7 4.8 fusion.57
  628.9 4.8 fusion.53
  633.7 41.7 %all-reduce.2 = (f32[896]{0:T(1024)}, f32[1152]{0:T(1024)}, f32[896]{0:T(1024)}) all-reduce(f32[896]{0:T(1024)S(1)} %get-tuple-element.236, f32[1152]{0:T(1024)S(1)} %convert_reduce_fusion, f32[896]{0:T(1024)S(1)} %get-tuple-element.234), channel_id=1, replica_groups=mesh['dp'=8,'mp'=4] {'dp','mp'}, use_global_device_ids=true, to_apply=%region_22.23 | all-reduce | flops 2944 | bytes 23552 | tf_op jit(solution)/shard_map/psum | solution.py:247
  675.4 3.3 fusion.49
  678.7 42.2 %reduce-scatter.16.cloned.1.call-done = f32[112,1216]{1,0:T(8,128)} async-done(((f32[896,1216]{1,0:T(8,128)}), f32[112,1216]{1,0:T(8,128)}) %reduce-scatter.16.cloned.1.call-update) | async-done | bytes 544784 | tf_op jit(solution)/shard_map/reduce_scatter | solution.py:209
  720.9 97.4 %reduce-scatter.18.cloned.1.call-done = f32[112,1216]{1,0:T(8,128)} async-done(((f32[896,1216]{1,0:T(8,128)}), f32[112,1216]{1,0:T(8,128)}) %reduce-scatter.18.cloned.1.call-update) | async-done | bytes 544784 | tf_op jit(solution)/shard_map/reduce_scatter | solution.py:210
  818.4 97.4 %reduce-scatter.20.cloned.1.call-done = f32[1216,112]{0,1:T(8,128)} async-done(((f32[1216,896]{0,1:T(8,128)}), f32[1216,112]{0,1:T(8,128)}) %reduce-scatter.20.cloned.1.call-update) | async-done | bytes 544784 | tf_op jit(solution)/shard_map/reduce_scatter | solution.py:211
  915.8 173.0 %all-reduce.6.cloned.1.call-done = (f32[896,1152]{1,0:T(8,128)}, f32[896,896]{1,0:T(8,128)}) async-done(((f32[896,1152]{1,0:T(8,128)}, f32[896,896]{1,0:T(8,128)}), (f32[896,1152]{1,0:T(8,128)}, f32[896,896]{1,0:T(8,128)})) %all-reduce.6.cloned.1.call-update) | async-done | bytes 7340048 | tf_op jit(solution)/shard_map/psum | solution.py:247
  1088.8 4.6 copy.84
  (298 shorter events, 227.4 us)
Async XLA Ops:
  7.2 247.4 %copy-start = (bf16[1216,896]{1,0:T(8,128)(2,1)S(1)}, bf16[1216,896]{1,0:T(8,128)(2,1)}, u32[]{:S(2)}) copy-start(bf16[1216,896]{1,0:T(8,128)(2,1)} %param.24) | copy-start | bytes 6537220
  7.2 214.3 %all-gather.3.cloned.1.call-start = ((), (), s32[]{:S(2)}) async-start(), calls=%async_computation.7 | async-start | bytes 4587520 | tf_op jit(solution)/shard_map/all_gather | solution.py:185
  8.8 4.8 copy-start.18
  9.5 4.1 copy-start.16
  13.7 1.4 copy-start.26
  16.6 13.8 %copy-start.12 = (f32[512,32]{0,1:T(8,128)}, f32[512,32]{0,1:T(8,128)S(1)}, u32[]{:S(2)}) copy-start(f32[512,32]{0,1:T(8,128)S(1)} %get-tuple-element.308) | copy-start | bytes 196612
  49.0 4.4 copy-start.7
  57.7 125.8 %copy-start.9 = (bf16[512,896]{1,0:T(8,128)(2,1)S(1)}, bf16[512,896]{1,0:T(8,128)(2,1)}, u32[]{:S(2)}) copy-start(bf16[512,896]{1,0:T(8,128)(2,1)} %param.15) | copy-start | bytes 2752516
  60.0 2.0 copy-start.2
  69.0 2.0 copy-start.2
  78.0 2.0 copy-start.2
  87.0 2.0 copy-start.2
  95.9 2.0 copy-start.2
  104.9 2.0 copy-start.2
  113.9 2.0 copy-start.2
  122.9 2.0 copy-start.2
  131.8 2.0 copy-start.2
  140.8 2.0 copy-start.2
  149.8 2.0 copy-start.2
  158.8 2.0 copy-start.2
  167.8 2.0 copy-start.2
  176.8 2.0 copy-start.2
  183.5 3.1 copy-start.20
  186.5 1.2 copy-start.5
  188.9 65.6 %all-gather.5.cloned.1.call-start = ((), (), s32[]{:S(2)}) async-start(), calls=%async_computation.9 | async-start | bytes 4587520 | tf_op jit(solution)/shard_map/all_gather | solution.py:196
  189.7 165.4 %reduce-scatter.10.cloned.1.call-start = ((), (), s32[]{:S(2)}) async-start(), calls=%async_computation.10 | async-start | bytes 9175040 | tf_op jit(solution)/shard_map/reduce_scatter | solution.py:202
  221.5 10.5 copy-start.21
  221.5 10.5 copy-start.23
  254.6 18.9 %copy-start.22 = (bf16[896,1216]{0,1:T(8,128)(2,1)S(1)}, bf16[896,1216]{0,1:T(8,128)(2,1)}, u32[]{:S(2)}) copy-start(bf16[896,1216]{0,1:T(8,128)(2,1)} %param.22) | copy-start | bytes 6537220
  273.5 7.9 copy-start.24
  273.5 7.9 copy-start.27
  289.5 110.0 %reduce-scatter.8.cloned.1.call-start = ((), (), s32[]{:S(2)}) async-start(), calls=%async_computation.8 | async-start | bytes 4587520 | tf_op jit(solution)/shard_map/reduce_scatter | solution.py:189
  299.2 55.9 %copy-start.6 = (f32[512,896]{1,0:T(8,128)S(1)}, f32[512,896]{1,0:T(8,128)}, u32[]{:S(2)}) copy-start(f32[512,896]{1,0:T(8,128)} %copy-done.5) | copy-start | bytes 5505028
  299.2 100.3 %copy-start.8 = (bf16[512,896]{1,0:T(8,128)(2,1)S(1)}, bf16[512,896]{1,0:T(8,128)(2,1)}, u32[]{:S(2)}) copy-start(bf16[512,896]{1,0:T(8,128)(2,1)} %param.25) | copy-start | bytes 2752516
  299.2 314.2 %reduce-scatter.14.cloned.1.call-start = ((), (), s32[]{:S(2)}) async-start(), calls=%async_computation.12 | async-start | bytes 1310720 | tf_op jit(solution)/shard_map/reduce_scatter | solution.py:234
  399.5 4.1 copy-start.25
  403.6 2.2 copy-start.3
  568.6 53.1 %reduce-scatter.12.cloned.1.call-start = ((), (), s32[]{:S(2)}) async-start(), calls=%async_computation.11 | async-start | bytes 1310720 | tf_op jit(solution)/shard_map/reduce_scatter | solution.py:233
  573.8 147.1 %reduce-scatter.16.cloned.1.call-start = ((), (), s32[]{:S(2)}) async-start(), calls=%async_computation.13 | async-start | bytes 5160960 | tf_op jit(solution)/shard_map/reduce_scatter | solution.py:209
  585.1 233.3 %reduce-scatter.18.cloned.1.call-start = ((), (), s32[]{:S(2)}) async-start(), calls=%async_computation.14 | async-start | bytes 5160960 | tf_op jit(solution)/shard_map/reduce_scatter | solution.py:210
  595.8 320.0 %reduce-scatter.20.cloned.1.call-start = ((), (), s32[]{:S(2)}) async-start(), calls=%async_computation.15 | async-start | bytes 5160960 | tf_op jit(solution)/shard_map/reduce_scatter | solution.py:211
  606.7 0.8 copy-start.13
  606.7 0.9 copy-start.15
  606.8 482.0 %all-reduce.6.cloned.1.call-start = ((), (), s32[]{:S(2)}) async-start(), calls=%async_computation.16 | async-start | bytes 14680064 | tf_op jit(solution)/shard_map/psum | solution.py:247
  607.6 2.9 copy-start.4
  607.6 2.9 copy-start.14
  610.6 12.1 %copy-start.10 = (bf16[512,896]{1,0:T(8,128)(2,1)S(1)}, bf16[512,896]{1,0:T(8,128)(2,1)}, u32[]{:S(2)}) copy-start(bf16[512,896]{1,0:T(8,128)(2,1)} %param.15) | copy-start | bytes 2752516
  610.6 12.1 %copy-start.17 = (f32[896]{0:T(1024)S(1)}, f32[896]{0:T(1024)}, u32[]{:S(2)}) copy-start(f32[896]{0:T(1024)} %copy-done.16) | copy-start | bytes 10756
  610.6 12.1 %copy-start.19 = (f32[512]{0:T(512)S(1)}, f32[512]{0:T(512)}, u32[]{:S(2)}) copy-start(f32[512]{0:T(512)} %copy-done.18) | copy-start | bytes 6148
  1088.8 4.6 copy-start.11
  1088.8 6.3 copy-start.1
Sparse Core Ops, SparseCore 0:
  189.1 32.3 all-gather.2
  223.0 31.5 all-gather.4
  289.6 65.4 reduce-scatter.9
  358.3 41.1 reduce-scatter.7
  568.7 24.8 reduce-scatter.13
  596.7 24.8 reduce-scatter.11
  625.8 95.0 reduce-scatter.15
  725.1 93.1 reduce-scatter.17
  822.6 93.1 reduce-scatter.19
  922.0 166.7 all-reduce.5
where the time goes:
time: 1110 us; the launch traced here: 1100 us
  waiting for transfers between devices  562 us (51%)
  matrix products  352 us (32%)
  local copies, waits for them, and re-layouts  65.2 us (6%)
  blocking collectives  57.7 us (5%)
  other arithmetic  47.7 us (4%)
  between operations  15 us (1%)
    psum x1, waiting for transfers between devices, on_device(): lax.psum((grad_attn_gain, grad_qkv_weight, grad_qkv_bias, grad_out_weight...  173 us
    dot_general x47, matrix products, col_contract(): lax.dot_general(left_mat, right_mat, (((1,), (1,)), ((), ())), preferred_...  140 us
    reduce_scatter x1, waiting for transfers between devices, on_device(): lax.psum_scatter(grad_down, 'dp', scatter_dimension=1, tiled=True)  97.4 us
    reduce_scatter x1, waiting for transfers between devices, on_device(): lax.psum_scatter(grad_up, 'dp', scatter_dimension=0, tiled=True)  97.4 us
    dot_general x33, matrix products, row_contract(): lax.dot_general(left_mat, right_mat, (((0,), (0,)), ((), ())), preferred_...  89.4 us
    reduce_scatter x1, waiting for transfers between devices, on_device(): lax.psum_scatter(col_contract(grad_gate_act, gate_weight) + col_contract(...  55.8 us
    dot_general x14, matrix products, attend_head(): jnp.dot(attn_prob, value_head, preferred_element_type=jnp.float32)  54.7 us
    reduce_scatter x1, waiting for transfers between devices, on_device(): lax.psum_scatter(jnp.dot(hidden, down_weight, preferred_element_type=jnp....  42.4 us
  transfers between devices with their start and end apart: 10, of which 9 were waited for; matrix products, arithmetic and copies ran while one was open for 8% of the time, Pallas kernels for 0%

commit v1 on v0

v1 whole, which is shorter than its diff:
```python
import functools

import jax
import jax.numpy as jnp
from jax import lax
from jax.experimental import pallas as pl
from jax.experimental.pallas import tpu as pltpu
from jax.sharding import PartitionSpec as P

HEADS = 14
KV_HEADS = 2
HEAD = 64
MARKS = 16

norm_epsilon = 1e-06
rope_base = 1000000.0
masked_score = -1e30
vmem_bytes = 52 * 2**20


def dot(left, right, left_dim, right_dim):
    return lax.dot_general(
        left, right, (((left_dim,), (right_dim,)), ((), ())), preferred_element_type=jnp.float32
    )


def causal(tile):
    key_id = lax.broadcasted_iota(jnp.int32, tile.shape, 0)
    query_id = lax.broadcasted_iota(jnp.int32, tile.shape, 1)
    return jnp.where(key_id <= query_id, tile, masked_score)

def attend_kernel(bounds, q_ref, mark_ref, k_ref, v_ref, out_ref, log_ref, q_ext, acc, top):
    rows = q_ref.shape[1]
    half = rows // 2
    q_ext[0:HEAD, :] = q_ref[...]
    q_ext[HEAD:, :] = mark_ref[...]
    acc[...] = jnp.zeros_like(acc)
    top[...] = jnp.full_like(top, 2*masked_score)
    def tile(start, size, lo, hi, diag):
        keys = k_ref[0, pl.ds(start, size), :]
        scores = dot(keys, q_ext[:, lo:hi], 1, 0)
        if diag: scores = causal(scores)
        old = top[:, lo:hi]
        new = jnp.maximum(old, jnp.max(scores, axis=0, keepdims=True))
        weights = jnp.exp(scores - new).astype(jnp.bfloat16)
        top[:, lo:hi] = new
        acc[:, lo:hi] = acc[:, lo:hi]*jnp.exp(old-new) + dot(v_ref[0, :, pl.ds(start,size)], weights, 1, 0)
    first, own = bounds[0], bounds[1]
    def full(c, carry):
        tile(pl.multiple_of(c*rows, rows), rows, 0, rows, False)
        return carry
    lax.fori_loop(first, own, full, 0)
    base = pl.multiple_of(own*rows, rows)
    tile(base, half, half, rows, False)
    tile(base, half, 0, half, True)
    tile(pl.multiple_of(base+half, half), half, half, rows, True)
    total = acc[HEAD:HEAD+1, :]
    out_ref[...] = (acc[0:HEAD, :] / total).astype(jnp.bfloat16)
    log_ref[0] = top[...] + jnp.log(total)

def attend(bounds, q, marks_in, k, v):
    width, rows = q.shape
    heads = width // HEAD
    kv_heads, group, depth = k.shape
    rep = heads // kv_heads
    vd = v.shape[1]
    return pl.pallas_call(
        attend_kernel,
        grid_spec=pltpu.PrefetchScalarGridSpec(
            num_scalar_prefetch=1, grid=(heads,),
            in_specs=[
                pl.BlockSpec((HEAD, rows), lambda h, b: (h, 0)),
                pl.BlockSpec((MARKS, rows), lambda h, b: (0, 0)),
                pl.BlockSpec((1, group, depth), lambda h, b: (h // rep, 0, 0)),
                pl.BlockSpec((1, vd, group), lambda h, b: (h // rep, 0, 0)),
            ],
            out_specs=[
                pl.BlockSpec((HEAD, rows), lambda h, b: (h, 0)),
                pl.BlockSpec((1, 1, rows), lambda h, b: (h, 0, 0)),
            ],
            scratch_shapes=[pltpu.VMEM((depth, rows), jnp.bfloat16), pltpu.VMEM((vd, rows), jnp.float32), pltpu.VMEM((1, rows), jnp.float32)],
        ),
        out_shape=[jax.ShapeDtypeStruct((width, rows), jnp.bfloat16), jax.ShapeDtypeStruct((heads, 1, rows), jnp.float32)],
        compiler_params=pltpu.CompilerParams(vmem_limit_bytes=vmem_bytes),
        name="attend",
    )(bounds, q, marks_in, k, v)

def attend_back_kernel(bounds, q_ref, mark_ref, k_ref, kt_ref, vk_ref, o_ref, go_ref, log_ref, gq_ref, gk_ref, gv_ref, q_ext, acc, delta, *, rep):
    rows = q_ref.shape[1]
    half = rows // 2
    h = pl.program_id(0)
    q_ext[0:HEAD, :] = q_ref[...]
    q_ext[HEAD:, :] = mark_ref[...]
    acc[...] = jnp.zeros_like(acc)
    delta[...] = jnp.sum(o_ref[...].astype(jnp.float32)*go_ref[...].astype(jnp.float32), axis=0, keepdims=True)
    @pl.when(h % rep == 0)
    def _():
        gk_ref[...] = jnp.zeros_like(gk_ref)
        gv_ref[...] = jnp.zeros_like(gv_ref)
    def tile(start, size, lo, hi, diag):
        keys = k_ref[0, pl.ds(start, size), :]
        scores = dot(keys, q_ext[:, lo:hi], 1, 0)
        if diag: scores = causal(scores)
        prob = jnp.exp(scores - log_ref[0, :, lo:hi])
        go = go_ref[:, lo:hi]
        gprob = dot(vk_ref[0, pl.ds(start, size), :], go, 1, 0)
        gscore = (prob*(gprob - delta[:, lo:hi])).astype(jnp.bfloat16)
        prob = prob.astype(jnp.bfloat16)
        gv_ref[0, :, pl.ds(start, size)] += dot(go, prob, 1, 1)
        gk_ref[0, :, pl.ds(start, size)] += dot(q_ref[:, lo:hi], gscore, 1, 1)
        acc[:, lo:hi] += dot(kt_ref[0, :, pl.ds(start, size)], gscore, 1, 0)
    first, own = bounds[0], bounds[1]
    def full(c, carry):
        tile(pl.multiple_of(c*rows, rows), rows, 0, rows, False)
        return carry
    lax.fori_loop(first, own, full, 0)
    base = pl.multiple_of(own*rows, rows)
    tile(base, half, half, rows, False)
    tile(base, half, 0, half, True)
    tile(pl.multiple_of(base+half, half), half, half, rows, True)
    gq_ref[...] = acc[...]

def attend_back(bounds, q, marks_in, k, kt, vk, o, go, log):
    width, rows = q.shape
    heads = width // HEAD
    kv_heads, group, depth = k.shape
    rep = heads // kv_heads
    gshape = (kv_heads, HEAD, group)
    per_head = pl.BlockSpec((HEAD, rows), lambda h, b: (h, 0))
    def per_kv(shape): return pl.BlockSpec((1,)+tuple(shape[1:]), lambda h, b: (h // rep, 0, 0))
    return pl.pallas_call(
        functools.partial(attend_back_kernel, rep=rep),
        grid_spec=pltpu.PrefetchScalarGridSpec(
            num_scalar_prefetch=1, grid=(heads,),
            in_specs=[per_head, pl.BlockSpec((MARKS, rows), lambda h, b: (0, 0)), per_kv(k.shape), per_kv(kt.shape), per_kv(vk.shape), per_head, per_head, pl.BlockSpec((1, 1, rows), lambda h, b: (h, 0, 0))],
            out_specs=[per_head, per_kv(gshape), per_kv(gshape)],
            scratch_shapes=[pltpu.VMEM((depth, rows), jnp.bfloat16), pltpu.VMEM((HEAD, rows), jnp.float32), pltpu.VMEM((1, rows), jnp.float32)],
        ),
        out_shape=[jax.ShapeDtypeStruct((width, rows), jnp.float32), jax.ShapeDtypeStruct(gshape, jnp.float32), jax.ShapeDtypeStruct(gshape, jnp.float32)],
        compiler_params=pltpu.CompilerParams(vmem_limit_bytes=vmem_bytes),
        name="attend_back",
    )(bounds, q, marks_in, k, kt, vk, o, go, log)


def act_kernel(x_ref, cot_ref, gate_ref, up_ref, down_ref, out_ref, grad_ref, hid_ref, gg_ref, gu_ref):
    width = gate_ref.shape[1]
    step = 640 if width > 768 else width
    x = x_ref[...]
    cot = cot_ref[...]
    out = None
    for lo in range(0, width, step):
        cols = slice(lo, min(lo + step, width))
        gate = dot(x, gate_ref[:, cols], 1, 0)
        up = dot(x, up_ref[:, cols], 1, 0)
        grad_hidden = dot(cot, down_ref[cols, :], 1, 1)
        sig = jax.nn.sigmoid(gate)
        silu = gate * sig
        hidden = (silu * up).astype(jnp.bfloat16)
        grad_gate = (grad_hidden * up * (sig * (1.0 + gate * (1.0 - sig)))).astype(jnp.bfloat16)
        grad_up = (grad_hidden * silu).astype(jnp.bfloat16)
        hid_ref[:, cols] = hidden
        gg_ref[:, cols] = grad_gate
        gu_ref[:, cols] = grad_up
        part = dot(hidden, down_ref[cols, :], 1, 0)
        grad = dot(grad_gate, gate_ref[:, cols], 1, 1) + dot(grad_up, up_ref[:, cols], 1, 1)
        out = part if out is None else out + part
        total = grad if lo == 0 else total + grad
    out_ref[...] = out.astype(jnp.bfloat16)
    grad_ref[...] = total.astype(jnp.bfloat16)


def feed_forward(x, cot, gate_weight, up_weight, down_weight):
    rows, width = x.shape
    units = gate_weight.shape[1]
    tile = min(256, rows)
    by_rows = lambda cols: pl.BlockSpec((tile, cols), lambda i: (i, 0))
    whole = lambda w: pl.BlockSpec(w.shape, lambda i: (0, 0), pipeline_mode=pl.Buffered(1))
    shape = lambda cols: jax.ShapeDtypeStruct((rows, cols), jnp.bfloat16)
    return pl.pallas_call(
        act_kernel,
        grid=(rows // tile,),
        in_specs=[by_rows(width), by_rows(width), whole(gate_weight), whole(up_weight), whole(down_weight)],
        out_specs=[by_rows(width), by_rows(width), by_rows(units), by_rows(units), by_rows(units)],
        out_shape=[shape(width), shape(width), shape(units), shape(units), shape(units)],
        compiler_params=pltpu.CompilerParams(vmem_limit_bytes=vmem_bytes),
        cost_estimate=pl.CostEstimate(
            flops=12 * rows * width * units, bytes_accessed=6 * width * units + 6 * rows * units, transcendentals=rows * units
        ),
        name="feed_forward",
    )(x, cot, gate_weight, up_weight, down_weight)


def weight_kernel(*refs, groups, steps):
    out_ref, acc = refs[-2:]
    i = pl.program_id(0)

    @pl.when(i == 0)
    def _():
        acc[...] = jnp.zeros_like(acc)

    for g in range(groups):

        @pl.when(i // steps == g)
        def _():
            acc[...] += dot(refs[2 * g][...], refs[2 * g + 1][...], 0, 0)

    @pl.when(i == groups * steps - 1)
    def _():
        out_ref[...] = acc[...].astype(jnp.bfloat16)


def weight_grad(lefts, rights):
    rows, width = lefts[0].shape
    units = rights[0].shape[1]
    groups = len(lefts)
    tile = min(512, rows)
    steps = rows // tile
    args, specs = [], []
    for g in range(groups):
        place = lambda i, g=g: (jnp.clip(i - g * steps, 0, steps - 1), 0)
        args += [lefts[g], rights[g]]
        specs += [pl.BlockSpec((tile, width), place), pl.BlockSpec((tile, units), place)]
    return pl.pallas_call(
        functools.partial(weight_kernel, groups=groups, steps=steps),
        grid=(groups * steps,),
        in_specs=specs,
        out_specs=pl.BlockSpec((width, units), lambda i: (0, 0), pipeline_mode=pl.Buffered(1)),
        out_shape=jax.ShapeDtypeStruct((width, units), jnp.bfloat16),
        scratch_shapes=[pltpu.VMEM((width, units), jnp.float32)],
        compiler_params=pltpu.CompilerParams(vmem_limit_bytes=vmem_bytes),
        cost_estimate=pl.CostEstimate(
            flops=2 * groups * rows * width * units,
            bytes_accessed=2 * (groups * rows * (width + units) + width * units),
            transcendentals=0,
        ),
        name="weight_grad",
    )(*args)


def layout(length_row, positions):
    seq_ends = jnp.cumsum(length_row)
    segment = jnp.sum((positions[:, None] >= seq_ends[None, :]).astype(jnp.int32), axis=1)
    starts = seq_ends - length_row
    slot_ids = jnp.arange(length_row.shape[0], dtype=jnp.int32)
    seq_begin = jnp.sum(
        jnp.where(segment[:, None] == slot_ids[None, :], starts[None, :], 0), axis=1
    )
    return (segment, positions - seq_begin)


def rotate(values, cos_table, sin_table):
    rows = values.shape[1]
    halves = values.reshape(-1, 2, HEAD // 2, rows)
    lower, upper = halves[:, 0], halves[:, 1]
    turned = jnp.stack(
        [lower * cos_table - upper * sin_table, upper * cos_table + lower * sin_table], axis=1
    )
    return turned.reshape(-1, rows)


def rms_apply(values, gain_vec):
    inverse = lax.rsqrt(jnp.mean(values * values, axis=-1, keepdims=True) + norm_epsilon)
    return (values * inverse * gain_vec, inverse)


def rms_back(values, inverse, gain_vec, grad_out):
    scaled = grad_out * gain_vec
    mean_dot = jnp.mean(values * scaled, axis=-1, keepdims=True)
    grad_in = inverse * scaled - values * inverse * inverse * inverse * mean_dot
    grad_gain = jnp.sum(grad_out * values * inverse, axis=0)
    return (grad_in, grad_gain)


def after(value, earlier):
    return lax.optimization_barrier((value, earlier))[0]


def swap(value, axis, bit):
    count = lax.axis_size(axis)
    return lax.ppermute(value, axis, [(i, i ^ bit) for i in range(count)])


def high_bits(count):
    bits, bit = [], 2
    while bit < count:
        bits.append(bit)
        bit *= 2
    return bits


def spread_far(value):
    blocks = {0: value}
    for bit in high_bits(lax.axis_size("mp")):
        for offset in sorted(blocks):
            blocks[offset | bit] = swap(blocks[offset], "mp", bit)
    return blocks


def collect_near(parts):
    return {
        offset: parts[offset].astype(jnp.float32) + swap(parts[offset | 1], "mp", 1).astype(jnp.float32)
        for offset in parts
        if offset % 2 == 0
    }


def collect_far(parts):
    for bit in high_bits(lax.axis_size("mp")):
        parts = {
            offset: parts[offset] + swap(parts[offset | bit].astype(jnp.bfloat16), "mp", bit).astype(jnp.float32)
            for offset in parts
            if not offset & bit
        }
    return parts[0]


def halve(parts, axis, bit):
    mine = lax.rem(lax.axis_index(axis) // bit, 2)
    pairs = parts.reshape((parts.shape[0] // 2, 2) + parts.shape[1:])
    sent = lax.dynamic_index_in_dim(pairs, 1 - mine, 1, keepdims=False).astype(jnp.bfloat16)
    kept = lax.dynamic_index_in_dim(pairs, mine, 1, keepdims=False)
    return kept.astype(jnp.float32) + swap(sent, axis, bit).astype(jnp.float32)


def double(parts, axis, bit):
    mine = lax.rem(lax.axis_index(axis) // bit, 2)
    other = swap(parts, axis, bit)
    pairs = jnp.stack([jnp.where(mine == 0, parts, other), jnp.where(mine == 0, other, parts)], axis=1)
    return pairs.reshape((-1,) + parts.shape[1:])


def all_bits(count):
    return [1] + high_bits(count) if count > 1 else []


def scatter_dp(value):
    count = lax.axis_size("dp")
    parts = value.reshape(count, value.shape[0] // count, value.shape[1])
    for bit in all_bits(count):
        parts = halve(parts, "dp", bit)
    return parts[0]


def sum_everywhere(value):
    dp_count, mp_count = lax.axis_size("dp"), lax.axis_size("mp")
    rows, cols = value.shape
    share = -(-rows // (dp_count * mp_count))
    padded = jnp.pad(value, ((0, share * dp_count * mp_count - rows), (0, 0)))
    parts = padded.reshape(mp_count, dp_count * share, cols)
    for bit in all_bits(mp_count):
        parts = halve(parts, "mp", bit)
    pieces = parts.astype(jnp.bfloat16).reshape(dp_count, share, cols)
    for bit in all_bits(dp_count):
        pieces = halve(pieces, "dp", bit)
    pieces = pieces.astype(jnp.bfloat16)
    for bit in reversed(all_bits(dp_count)):
        pieces = double(pieces, "dp", bit)
    parts = pieces.reshape(1, dp_count * share, cols)
    for bit in reversed(all_bits(mp_count)):
        parts = double(parts, "mp", bit)
    return parts.reshape(-1, cols)[:rows].astype(jnp.float32)


def on_device(
    tokens,
    seq_lengths,
    attn_gain,
    qkv_weight,
    qkv_bias,
    out_weight,
    mlp_gain,
    gate_weight,
    up_weight,
    down_weight,
    cotangent,
):
    tok_rows, width = tokens.shape
    mp_count = lax.axis_size("mp")
    mp_index = lax.axis_index("mp")
    group_rows = tok_rows * mp_count
    q_width = HEADS * HEAD
    kv_width = KV_HEADS * HEAD
    score_scale = HEAD ** (-0.5)
    row_base = mp_index * tok_rows
    lengths = seq_lengths[0]
    own_rows = row_base + jnp.arange(tok_rows, dtype=jnp.int32)
    segment, position = layout(lengths, own_rows)
    key_segment, _ = layout(lengths, jnp.arange(group_rows, dtype=jnp.int32))
    bounds = jnp.stack([(row_base - position[0]) // tok_rows, mp_index]).astype(jnp.int32)
    marks = jnp.arange(MARKS, dtype=jnp.int32)
    query_marks = (segment[None, :] != marks[:, None]).astype(jnp.bfloat16)
    key_marks = jnp.where(key_segment[:, None] == marks[None, :], masked_score, 0.0).astype(jnp.bfloat16)
    inverse_freq = rope_base ** (-2.0 * jnp.arange(HEAD // 2, dtype=jnp.float32) / HEAD)
    angles = inverse_freq[:, None] * position.astype(jnp.float32)[None, :]
    cos_table, sin_table = jnp.cos(angles), jnp.sin(angles)

    inputs = tokens.astype(jnp.float32)
    attn_scale = attn_gain.astype(jnp.float32)
    normed_full, inverse_one = rms_apply(inputs, attn_scale)
    normed = normed_full.astype(jnp.bfloat16)
    projected = dot(qkv_weight, normed, 0, 1) + qkv_bias.astype(jnp.float32)[:, None]
    queries = rotate(projected[:q_width], cos_table, sin_table).astype(jnp.bfloat16) * jnp.bfloat16(score_scale)
    keys_own = rotate(projected[q_width : q_width + kv_width], cos_table, sin_table)
    own_kv = jnp.concatenate([keys_own, projected[q_width + kv_width :]], axis=0).astype(jnp.bfloat16)

    far = spread_far(own_kv)
    offsets = sorted(far)
    near = swap(jnp.stack([far[o] for o in offsets]), "mp", 1)
    blocks = {}
    for i, o in enumerate(offsets):
        blocks[o], blocks[o | 1] = far[o], near[i]
    for bit in all_bits(mp_count):
        mine = lax.rem(mp_index // bit, 2) == 0
        for o in range(mp_count):
            if not o & bit:
                low, high = blocks[o], blocks[o | bit]
                blocks[o], blocks[o | bit] = jnp.where(mine, low, high), jnp.where(mine, high, low)
    group_kv = jnp.concatenate([blocks[o] for o in range(mp_count)], axis=1)
    keys_t = group_kv[:kv_width].reshape(KV_HEADS, HEAD, group_rows)
    values_t = group_kv[kv_width:].reshape(KV_HEADS, HEAD, group_rows)
    keys = keys_t.transpose(0, 2, 1)
    values = values_t.transpose(0, 2, 1)
    marked_keys = jnp.concatenate([keys, jnp.broadcast_to(key_marks, (KV_HEADS,) + key_marks.shape)], axis=2)
    marked_values = jnp.concatenate([values_t, jnp.ones((KV_HEADS, MARKS, group_rows), jnp.bfloat16)], axis=1)

    cot_far = spread_far(after(cotangent, group_kv))
    cot_near = {o | 1: swap(cot_far[o], "mp", 1) for o in cot_far}
    cots = {**cot_far, **cot_near}

    attended, log_totals = attend(bounds, queries, query_marks, marked_keys, marked_values)
    middle = inputs + dot(attended, out_weight, 0, 0)
    mlp_scale = mlp_gain.astype(jnp.float32)
    normed_mid_full, inverse_two = rms_apply(middle, mlp_scale)
    normed_mid = normed_mid_full.astype(jnp.bfloat16)

    mids = spread_far(normed_mid)
    mids.update({o | 1: swap(mids[o], "mp", 1) for o in sorted(mids)})
    xs, cs, hids, ggs, gus = [], [], [], [], []
    outs, grads = {}, {}
    for o in range(0, mp_count, 2):
        x = jnp.concatenate([mids[o], mids[o | 1]], axis=0)
        c = jnp.concatenate([cots[o], cots[o | 1]], axis=0)
        out, grad, hid, gg, gu = feed_forward(x, c, gate_weight, up_weight, down_weight)
        xs.append(x), cs.append(c), hids.append(hid), ggs.append(gg), gus.append(gu)
        for k in (0, 1):
            outs[o | k] = out[k * tok_rows : (k + 1) * tok_rows]
            grads[o | k] = grad[k * tok_rows : (k + 1) * tok_rows]
    grad_normed_mid = collect_far(collect_near(grads))
    wide_gate = weight_grad(xs, ggs)
    wide_up = weight_grad(xs, gus)
    wide_down = weight_grad(cs, hids)
    grad_gate = scatter_dp(wide_gate)
    grad_up = scatter_dp(wide_up)
    grad_down = scatter_dp(wide_down).T
    mlp_out = collect_far(collect_near(after(outs, grad_normed_mid)))
    output = (middle + mlp_out).astype(jnp.bfloat16)

    grad_from_mid, grad_mlp_gain = rms_back(middle, inverse_two, mlp_scale, grad_normed_mid)
    grad_middle = cotangent.astype(jnp.float32) + grad_from_mid
    grad_branch = grad_middle.astype(jnp.bfloat16)
    grad_attended = dot(out_weight, grad_branch, 1, 1).astype(jnp.bfloat16)
    grad_queries, grad_keys, grad_values = attend_back(
        bounds, queries, query_marks, marked_keys, keys_t, values, attended, grad_attended, log_totals
    )
    grad_out_weight = sum_everywhere(dot(attended, grad_branch, 1, 0))

    grad_kv = jnp.concatenate([grad_keys.reshape(kv_width, group_rows), grad_values.reshape(kv_width, group_rows)], axis=0)
    kv_parts = {
        o: lax.dynamic_slice_in_dim(grad_kv, (mp_index ^ o) * tok_rows, tok_rows, 1).astype(jnp.bfloat16)
        for o in range(mp_count)
    }
    own_grad_kv = collect_far(collect_near(kv_parts))
    back_q = rotate(grad_queries * score_scale, cos_table, -sin_table)
    back_k = rotate(own_grad_kv[:kv_width], cos_table, -sin_table)
    grad_projected = jnp.concatenate([back_q, back_k, own_grad_kv[kv_width:]], axis=0).astype(jnp.bfloat16)
    grad_normed = dot(grad_projected, qkv_weight, 0, 1)
    grad_qkv = dot(normed, grad_projected, 0, 1)
    grad_bias = jnp.sum(grad_projected.astype(jnp.float32), axis=1)
    grad_from_first, grad_attn_gain = rms_back(inputs, inverse_one, attn_scale, grad_normed)
    grad_tokens = grad_middle + grad_from_first

    bias_cols = -(-grad_bias.shape[0] // width)
    bias_block = jnp.pad(grad_bias, (0, bias_cols * width - grad_bias.shape[0])).reshape(bias_cols, width)
    extra = jnp.concatenate([grad_attn_gain[None], grad_mlp_gain[None], bias_block], axis=0)
    extra = jnp.pad(extra, ((0, 128 - extra.shape[0]), (0, 0))).T
    summed = sum_everywhere(jnp.concatenate([grad_qkv, extra], axis=1))
    qkv_cols = grad_qkv.shape[1]
    sums = summed[:, qkv_cols : qkv_cols + 2 + bias_cols].T
    return (
        output,
        grad_tokens,
        sums[0],
        summed[:, :qkv_cols],
        sums[2:].reshape(-1)[: grad_bias.shape[0]],
        grad_out_weight,
        sums[1],
        grad_gate,
        grad_up,
        grad_down,
    )


def solution(mesh):
    return jax.shard_map(
        on_device,
        mesh=mesh,
        in_specs=(
            P(("dp", "mp"), None),
            P("dp", None),
            P(),
            P(),
            P(),
            P(),
            P(),
            P(None, "mp"),
            P(None, "mp"),
            P("mp", None),
            P(("dp", "mp"), None),
        ),
        out_specs=(
            P(("dp", "mp"), None),
            P(("dp", "mp"), None),
            P(),
            P(),
            P(),
            P(),
            P(),
            P("dp", "mp"),
            P("dp", "mp"),
            P("mp", "dp"),
        ),
        check_vma=False,
    )
```

time: 1110 us -> 490 us (0.44)
  waiting for transfers between devices: 562 us -> 132 us
  matrix products: 352 us -> 14.6 us
  Pallas kernels: 0 us -> 112 us
  starting transfers between devices: 1.51 us -> 107 us
  blocking collectives: 57.7 us -> 0 us
  between operations: 15 us -> 2.87 us
    reduce_scatter x7 -> x0, waiting for transfers between devices: 343 us -> none  [the longest x1 97.4 us: on_device(): lax.psum_scatter(grad_down, 'dp', scatter_dimension=1, tiled=True)]
    dot_general x113 -> x6, matrix products: 352 us -> 14.6 us  [dot(): lax.dot_general(left, right, (((left_dim,), (right_dim,)), ((), ())), pre...]
    psum x1 -> x0, waiting for transfers between devices: 173 us -> none  [on_device(): lax.psum((grad_attn_gain, grad_qkv_weight, grad_qkv_bias, grad_out_weight...]
    ppermute x0 -> x46, waiting for transfers between devices: none -> 132 us  [swap(): return lax.ppermute(value, axis, [(i, i ^ bit) for i in range(count)])]
    pallas_call x0 -> x7, Pallas kernels: none -> 112 us  [the longest x2 49.5 us: feed_forward(): pl.pallas_call(act_kernel, grid=(rows // tile,), in_specs=[by_rows(width)...]
    ppermute x0 -> x46, starting transfers between devices: none -> 107 us  [swap(): return lax.ppermute(value, axis, [(i, i ^ bit) for i in range(count)])]
    all_gather x2 -> x0, waiting for transfers between devices: 46.1 us -> none  [the longest x1 31.3 us: on_device(): gathered = lax.all_gather(normed_mid, 'mp', axis=0, tiled=True)]
    psum x1 -> x0, blocking collectives: 41.7 us -> none  [on_device(): lax.psum((grad_attn_gain, grad_qkv_weight, grad_qkv_bias, grad_out_weight...]
  transfers between devices with their start and end apart: 10 -> 46, of which waited for: 9 -> 20; matrix products, arithmetic and copies ran while one was open for 8% -> 20% of each run, Pallas kernels for 0% -> 20%
where the time goes in v1:
time: 490 us; the launch traced here: 485 us
  waiting for transfers between devices  132 us (27%)
  Pallas kernels  112 us (23%)
  starting transfers between devices  107 us (22%)
  local copies, waits for them, and re-layouts  68.5 us (14%)
  other arithmetic  48.2 us (10%)
  matrix products  14.6 us (3%)
    ppermute x46, waiting for transfers between devices, swap(): return lax.ppermute(value, axis, [(i, i ^ bit) for i in range(count)])  132 us
    ppermute x46, starting transfers between devices, swap(): return lax.ppermute(value, axis, [(i, i ^ bit) for i in range(count)])  107 us
    pallas_call x2, Pallas kernels, feed_forward(): pl.pallas_call(act_kernel, grid=(rows // tile,), in_specs=[by_rows(width)...  49.5 us
    pallas_call x3, Pallas kernels, weight_grad(): pl.pallas_call(functools.partial(weight_kernel, groups=groups, steps=step...  29.9 us
    unnamed x121, local copies, waits for them, and re-layouts  21.9 us
    pallas_call x1, Pallas kernels, attend_back(): pl.pallas_call(functools.partial(attend_back_kernel, rep=rep), grid_spec=...  17.2 us
    pallas_call x1, Pallas kernels, attend(): pl.pallas_call(attend_kernel, grid_spec=pltpu.PrefetchScalarGridSpec(num_...  15.3 us
    dot_general x6, matrix products, dot(): lax.dot_general(left, right, (((left_dim,), (right_dim,)), ((), ())), pre...  14.6 us
  transfers between devices with their start and end apart: 46, of which 20 were waited for; matrix products, arithmetic and copies ran while one was open for 20% of the time, Pallas kernels for 20%

profile of v1, /device:TPU:0, one launch (start us, length us, event | category | flops | bytes accessed | tf_op | source)
XLA Modules:
  0.0 485.3 jit_solution(884620838852249678)
XLA Ops:
  3.7 2.7 fusion
  10.3 3.0 collective-permute-start
  13.2 2.8 slice.129
  16.1 2.9 copy.127
  26.1 1.8 collective-permute-done.1
  34.9 15.3 %attend.1 = (bf16[896,512]{1,0:T(8,128)(2,1)S(1)}, f32[14,1,512]{2,1,0:T(1,128)S(1)}) custom-call(s32[2]{0:T(128)S(1)} %pad_add_fusion.bounds, bf16[896,512]{1,0:T(8,128)(2,1)} %bitcast.234, bf16[16,512]{1,0:T(8,128)(2,1)S(1)} %fusion.34.mark_ref, bf16[2,2048,80]{2,1,0:T(8,128)(2,1)} %copy.133.k_ref, bf16[2,80,2048]{2,1,0:T(8,128)(2,1)S(1)} %concatenate.58.v_ref), custom_call_target="tpu_custom_call" | custom-call | tf_op jit(solution)/shard_map/attend/pallas_call | solution.py:67
  54.0 16.5 %collective-permute-start.4 = (bf16[512,896]{1,0:T(8,128)(2,1)}, bf16[512,896]{1,0:T(8,128)(2,1)}, u32[]{:S(2)}, u32[]{:S(2)}) collective-permute-start(bf16[512,896]{1,0:T(8,128)(2,1)} %multiply_convert_fusion), channel_id=1, source_target_pairs={{0,2},{1,3},{2,0},{3,1},{4,6},{5,7},{6,4},{7,5},{8,10},{9,11},{10,... | collective-permute-start | bytes 2752520 | tf_op jit(solution)/shard_map/ppermute | solution.py:280
  70.5 8.3 %collective-permute-start.2 = (bf16[512,896]{1,0:T(8,128)(2,1)}, bf16[512,896]{1,0:T(8,128)(2,1)}, u32[]{:S(2)}, u32[]{:S(2)}) collective-permute-start(bf16[512,896]{1,0:T(8,128)(2,1)} %multiply_convert_fusion), channel_id=1, source_target_pairs={{0,1},{1,0},{2,3},{3,2},{4,5},{5,4},{6,7},{7,6},{8,9},{9,8},{10,11... | collective-permute-start | bytes 2752520 | tf_op jit(solution)/shard_map/ppermute | solution.py:280
  78.9 4.2 copy.134.gate_ref
  83.0 4.1 copy.135.up_ref
  87.2 2.4 copy.138
  90.8 9.3 %collective-permute-start.5 = (bf16[512,896]{1,0:T(8,128)(2,1)}, bf16[512,896]{1,0:T(8,128)(2,1)S(1)}, u32[]{:S(2)}, u32[]{:S(2)}) collective-permute-start(bf16[512,896]{1,0:T(8,128)(2,1)} %collective-permute-done.4), channel_id=1, source_target_pairs={{0,1},{1,0},{2,3},{3,2},{4,5},{5,4},{6,7},{7,6},{8,9},{9,8},{10,11... | collective-permute-start | bytes 2752520 | tf_op jit(solution)/shard_map/ppermute | solution.py:280
  100.1 3.6 collective-permute-done.6
  103.7 7.8 %collective-permute-start.7 = (bf16[512,896]{1,0:T(8,128)(2,1)}, bf16[512,896]{1,0:T(8,128)(2,1)S(1)}, u32[]{:S(2)}, u32[]{:S(2)}) collective-permute-start(bf16[512,896]{1,0:T(8,128)(2,1)} %collective-permute-done.6), channel_id=1, source_target_pairs={{0,1},{1,0},{2,3},{3,2},{4,5},{5,4},{6,7},{7,6},{8,9},{9,8},{10,11... | collective-permute-start | bytes 2752520 | tf_op jit(solution)/shard_map/ppermute | solution.py:280
  111.5 2.9 pad_maximum_fusion.1.x_ref.refs_0_
  116.9 24.6 %feed_forward.2 = (bf16[1024,896]{1,0:T(8,128)(2,1)S(1)}, bf16[1024,896]{1,0:T(8,128)(2,1)}, bf16[1024,1216]{1,0:T(8,128)(2,1)}, bf16[1024,1216]{1,0:T(8,128)(2,1)}, bf16[1024,1216]{1,0:T(8,128)(2,1)}) custom-call(bf16[1024,896]{1,0:T(8,128)(2,1)} %pad_maximum_fusion.1.x_ref.refs_0_, bf16[1024,896]{1,0:T(8,128)(2,1)} %copy-done.4, ...), custom_call_target="tpu_custom_call" | custom-call | flops 13388218368 | bytes 14008320 | tf_op jit(solution)/shard_map/feed_forward/pallas_call | solution.py:179
  141.5 2.2 slice.114
  145.0 2.2 constant_dynamic-update-slice_fusion.5
  149.8 24.9 %feed_forward.3 = (bf16[1024,896]{1,0:T(8,128)(2,1)S(1)}, bf16[1024,896]{1,0:T(8,128)(2,1)}, bf16[1024,1216]{1,0:T(8,128)(2,1)}, bf16[1024,1216]{1,0:T(8,128)(2,1)}, bf16[1024,1216]{1,0:T(8,128)(2,1)}) custom-call(bf16[1024,896]{1,0:T(8,128)(2,1)} %copy-done.42, bf16[1024,896]{1,0:T(8,128)(2,1)} %constant_dynamic-update-slice_fusion.4.cot_ref.refs_2_, ...), custom_call_target="tpu_custom_call" | custom-call | flops 13388218368 | bytes 14008320 | tf_op jit(solution)/shard_map/feed_forward/pallas_call | solution.py:179
  174.7 2.3 slice.116
  177.5 9.8 %weight_grad.3 = bf16[896,1216]{1,0:T(8,128)(2,1)} custom-call(bf16[1024,896]{1,0:T(8,128)(2,1)S(1)} %copy-done.3, bf16[1024,1216]{1,0:T(8,128)(2,1)} %get-tuple-element.44.refs_1_, bf16[1024,896]{1,0:T(8,128)(2,1)} %copy-done.42, bf16[1024,1216]{1,0:T(8,128)(2,1)} %get-tuple-element.45.refs_3_), custom_call_target="tpu_custom_call" | custom-call | flops 4462739456 | bytes 10829824 | tf_op jit(solution)/shard_map/weight_grad/pallas_call | solution.py:223
  187.3 2.3 dynamic-slice_bitcast_fusion.2
  189.7 2.0 collective-permute-start.37
  191.7 9.8 %weight_grad.4 = bf16[896,1216]{1,0:T(8,128)(2,1)} custom-call(bf16[1024,896]{1,0:T(8,128)(2,1)S(1)} %copy-done.3, bf16[1024,1216]{1,0:T(8,128)(2,1)} %get-tuple-element.46.refs_1_, bf16[1024,896]{1,0:T(8,128)(2,1)} %copy-done.42, bf16[1024,1216]{1,0:T(8,128)(2,1)} %get-tuple-element.47.refs_3_), custom_call_target="tpu_custom_call" | custom-call | flops 4462739456 | bytes 10829824 | tf_op jit(solution)/shard_map/weight_grad/pallas_call | solution.py:223
  203.3 10.2 %weight_grad.5 = bf16[896,1216]{1,0:T(8,128)(2,1)} custom-call(bf16[1024,896]{1,0:T(8,128)(2,1)S(1)} %copy-done.5, bf16[1024,1216]{1,0:T(8,128)(2,1)} %get-tuple-element.48.refs_1_, bf16[1024,896]{1,0:T(8,128)(2,1)} %constant_dynamic-update-slice_fusion.4.cot_ref.refs_2_, bf16[1024,1216]{1,0:T(8,128)(2,1)} %get-tuple-element.49.refs_3_), custom_call_target="tpu_custom_call" | custom-call | flops 4462739456 | bytes 10829824 | tf_op jit(solution)/shard_map/weight_grad/pallas_call | solution.py:223
  214.9 1.8 collective-permute-start.43
  219.6 2.1 collective-permute-start.10
  223.7 18.9 %collective-permute-done.40 = bf16[4,112,1216]{2,1,0:T(8,128)(2,1)S(1)} collective-permute-done((bf16[4,112,1216]{2,1,0:T(8,128)(2,1)S(1)}, bf16[4,112,1216]{2,1,0:T(8,128)(2,1)S(1)}, u32[]{:S(2)}, u32[]{:S(2)}) %collective-permute-start.40) | collective-permute-done | bytes 1089568 | tf_op jit(solution)/shard_map/ppermute | solution.py:280
  242.9 2.2 collective-permute-start.41
  245.1 21.4 %collective-permute-done.43 = bf16[4,112,1216]{2,1,0:T(8,128)(2,1)S(1)} collective-permute-done((bf16[4,112,1216]{2,1,0:T(8,128)(2,1)S(1)}, bf16[4,112,1216]{2,1,0:T(8,128)(2,1)S(1)}, u32[]{:S(2)}, u32[]{:S(2)}) %collective-permute-start.43) | collective-permute-done | bytes 1089568 | tf_op jit(solution)/shard_map/ppermute | solution.py:280
  266.8 2.7 multiply_reduce_fusion
  270.4 1.8 collective-permute-start.44
  273.2 2.6 collective-permute-start.39
  276.0 2.1 collective-permute-start.13
  280.0 19.1 %collective-permute-done.13 = bf16[512,896]{1,0:T(8,128)(2,1)S(1)} collective-permute-done((bf16[512,896]{1,0:T(8,128)(2,1)S(1)}, bf16[512,896]{1,0:T(8,128)(2,1)S(1)}, u32[]{:S(2)}, u32[]{:S(2)}) %collective-permute-start.13) | collective-permute-done | bytes 917536 | tf_op jit(solution)/shard_map/ppermute | solution.py:280
  299.1 3.1 subtract_add_fusion
  302.3 2.1 fusion.12.go_ref
  305.5 17.2 %attend_back.1 = (f32[896,512]{1,0:T(8,128)}, f32[2,64,2048]{2,1,0:T(8,128)}, f32[2,64,2048]{2,1,0:T(8,128)}) custom-call(s32[2]{0:T(128)S(1)} %pad_add_fusion.bounds, bf16[896,512]{1,0:T(8,128)(2,1)S(1)} %bitcast.235, bf16[16,512]{1,0:T(8,128)(2,1)S(1)} %fusion.34.mark_ref, bf16[2,2048,80]{2,1,0:T(8,128)(2,1)} %copy.133.k_ref, ...), custom_call_target="tpu_custom_call" | custom-call | tf_op jit(solution)/shard_map/attend_back/pallas_call | solution.py:131
  324.1 10.5 %collective-permute-start.15 = (bf16[256,512]{1,0:T(8,128)(2,1)S(1)}, bf16[256,512]{1,0:T(8,128)(2,1)S(1)}, u32[]{:S(2)}, u32[]{:S(2)}) collective-permute-start(bf16[256,512]{1,0:T(8,128)(2,1)S(1)} %get-tuple-element.62), channel_id=1, source_target_pairs={{0,1},{1,0},{2,3},{3,2},{4,5},{5,4},{6,7},{7,6},{8,9},{9,8},{10,11... | collective-permute-start | bytes 786440 | tf_op jit(solution)/shard_map/ppermute | solution.py:280
  336.6 23.2 %collective-permute-start.16 = (bf16[256,512]{1,0:T(8,128)(2,1)S(1)}, bf16[256,512]{1,0:T(8,128)(2,1)S(1)}, u32[]{:S(2)}, u32[]{:S(2)}) collective-permute-start(bf16[256,512]{1,0:T(8,128)(2,1)S(1)} %add_convert_fusion.7), channel_id=1, source_target_pairs={{0,2},{1,3},{2,0},{3,1},{4,6},{5,7},{6,4},{7,5},{8,10},{9,11},{10,... | collective-permute-start | bytes 786440 | tf_op jit(solution)/shard_map/ppermute | solution.py:280
  361.2 5.6 %collective-permute-done.16 = bf16[256,512]{1,0:T(8,128)(2,1)S(1)} collective-permute-done((bf16[256,512]{1,0:T(8,128)(2,1)S(1)}, bf16[256,512]{1,0:T(8,128)(2,1)S(1)}, u32[]{:S(2)}, u32[]{:S(2)}) %collective-permute-start.16) | collective-permute-done | bytes 262176 | tf_op jit(solution)/shard_map/ppermute | solution.py:280
  367.0 3.6 fusion.11
  370.9 3.6 fusion.29
  374.8 2.7 pad_maximum_fusion
  378.8 2.0 bitcast_add_fusion.1
  380.9 1.8 collective-permute-start.28
  385.0 7.6 %collective-permute-done.28 = bf16[1,224,896]{2,1,0:T(8,128)(2,1)S(1)} collective-permute-done((bf16[1,224,896]{2,1,0:T(8,128)(2,1)S(1)}, bf16[1,224,896]{2,1,0:T(8,128)(2,1)S(1)}, u32[]{:S(2)}, u32[]{:S(2)}) %collective-permute-start.28) | collective-permute-done | bytes 401440 | tf_op jit(solution)/shard_map/ppermute | solution.py:280
  393.4 1.8 reshape_reshape.33
  397.8 2.2 bitcast_add_fusion
  401.8 1.8 add_bitcast_fusion.2
  404.3 10.3 %collective-permute-done.18 = bf16[1,224,1280]{2,1,0:T(8,128)(2,1)S(1)} collective-permute-done((bf16[1,224,1280]{2,1,0:T(8,128)(2,1)S(1)}, bf16[1,224,1280]{2,1,0:T(8,128)(2,1)S(1)}, u32[]{:S(2)}, u32[]{:S(2)}) %collective-permute-start.18) | collective-permute-done | bytes 573472 | tf_op jit(solution)/shard_map/ppermute | solution.py:280
  416.9 6.3 %collective-permute-done.19 = bf16[4,28,1280]{2,1,0:T(8,128)(2,1)S(1)} collective-permute-done((bf16[4,28,1280]{2,1,0:T(8,128)(2,1)S(1)}, bf16[4,28,1280]{2,1,0:T(8,128)(2,1)S(1)}, u32[]{:S(2)}, u32[]{:S(2)}) %collective-permute-start.19) | collective-permute-done | bytes 286752 | tf_op jit(solution)/shard_map/ppermute | solution.py:280
  424.2 4.9 %collective-permute-done.20 = bf16[2,28,1280]{2,1,0:T(8,128)(2,1)S(1)} collective-permute-done((bf16[2,28,1280]{2,1,0:T(8,128)(2,1)S(1)}, bf16[2,28,1280]{2,1,0:T(8,128)(2,1)S(1)}, u32[]{:S(2)}, u32[]{:S(2)}) %collective-permute-start.20) | collective-permute-done | bytes 143392 | tf_op jit(solution)/shard_map/ppermute | solution.py:280
  430.6 6.3 %collective-permute-done.21 = bf16[1,28,1280]{2,1,0:T(8,128)(2,1)S(1)} collective-permute-done((bf16[1,28,1280]{2,1,0:T(8,128)(2,1)S(1)}, bf16[1,28,1280]{2,1,0:T(8,128)(2,1)S(1)}, u32[]{:S(2)}, u32[]{:S(2)}) %collective-permute-start.21) | collective-permute-done | bytes 71712 | tf_op jit(solution)/shard_map/ppermute | solution.py:280
  437.1 5.3 %collective-permute-done.22 = bf16[1,28,1280]{2,1,0:T(8,128)(2,1)S(1)} collective-permute-done((bf16[1,28,1280]{2,1,0:T(8,128)(2,1)S(1)}, bf16[1,28,1280]{2,1,0:T(8,128)(2,1)S(1)}, u32[]{:S(2)}, u32[]{:S(2)}) %collective-permute-start.22) | collective-permute-done | bytes 71712 | tf_op jit(solution)/shard_map/ppermute | solution.py:280
  444.2 3.7 collective-permute-done.23
  448.5 3.4 collective-permute-done.34
  457.6 2.0 reshape_reshape.31
  460.4 1.8 add_bitcast_fusion.1
  464.8 8.5 %collective-permute-done.25 = bf16[1,224,1280]{2,1,0:T(8,128)(2,1)S(1)} collective-permute-done((bf16[1,224,1280]{2,1,0:T(8,128)(2,1)}, bf16[1,224,1280]{2,1,0:T(8,128)(2,1)S(1)}, u32[]{:S(2)}, u32[]{:S(2)}) %collective-permute-start.25) | collective-permute-done | bytes 573472 | tf_op jit(solution)/shard_map/ppermute | solution.py:280
  473.6 2.0 add_bitcast_fusion
  475.7 1.8 fusion.7
  477.9 1.9 copy.150
  480.8 2.3 slice.148
  (312 shorter events, 80.3 us)
Async XLA Ops:
  9.3 9.7 %copy-start.37 = (f32[32,512]{1,0:T(8,128)}, f32[32,512]{1,0:T(8,128)S(1)}, u32[]{:S(2)}) copy-start(f32[32,512]{1,0:T(8,128)S(1)} %get-tuple-element.103) | copy-start | bytes 196612
  10.3 14.6 %collective-permute-start = (bf16[256,512]{0,1:T(8,128)(2,1)}, bf16[256,512]{0,1:T(8,128)(2,1)}, u32[]{:S(2)}, u32[]{:S(2)}) collective-permute-start(bf16[256,512]{0,1:T(8,128)(2,1)} %pad_maximum_fusion.10), channel_id=1, source_target_pairs={{0,2},{1,3},{2,0},{3,1},{4,6},{5,7},{6,4},{7,5},{8,10},{9,11},{10,... | collective-permute-start | bytes 786440 | tf_op jit(solution)/shard_map/ppermute | solution.py:280
  25.9 2.0 collective-permute-start.1
  34.1 16.1 %copy-start.18 = (bf16[512,896]{1,0:T(8,128)(2,1)S(1)}, bf16[512,896]{1,0:T(8,128)(2,1)}, u32[]{:S(2)}) copy-start(bf16[512,896]{1,0:T(8,128)(2,1)} %param.11) | copy-start | bytes 2752516
  34.1 16.1 %copy-start.55 = (bf16[896,896]{1,0:T(8,128)(2,1)S(1)}, bf16[896,896]{1,0:T(8,128)(2,1)}, u32[]{:S(2)}) copy-start(bf16[896,896]{1,0:T(8,128)(2,1)} %param.16) | copy-start | bytes 4816900
  50.2 254.2 %copy-start.2 = (bf16[896,512]{1,0:T(8,128)(2,1)}, bf16[896,512]{1,0:T(8,128)(2,1)S(1)}, u32[]{:S(2)}) copy-start(bf16[896,512]{1,0:T(8,128)(2,1)S(1)} %get-tuple-element.30.o_ref) | copy-start | bytes 2752516
  54.0 36.8 %collective-permute-start.4 = (bf16[512,896]{1,0:T(8,128)(2,1)}, bf16[512,896]{1,0:T(8,128)(2,1)}, u32[]{:S(2)}, u32[]{:S(2)}) collective-permute-start(bf16[512,896]{1,0:T(8,128)(2,1)} %multiply_convert_fusion), channel_id=1, source_target_pairs={{0,2},{1,3},{2,0},{3,1},{4,6},{5,7},{6,4},{7,5},{8,10},{9,11},{10,... | collective-permute-start | bytes 2752520 | tf_op jit(solution)/shard_map/ppermute | solution.py:280
  70.5 33.2 %collective-permute-start.6 = (bf16[512,896]{1,0:T(8,128)(2,1)}, bf16[512,896]{1,0:T(8,128)(2,1)}, u32[]{:S(2)}, u32[]{:S(2)}) collective-permute-start(bf16[512,896]{1,0:T(8,128)(2,1)} %param.21), channel_id=1, source_target_pairs={{0,2},{1,3},{2,0},{3,1},{4,6},{5,7},{6,4},{7,5},{8,10},{9,11},{10,... | collective-permute-start | bytes 2752520 | tf_op jit(solution)/shard_map/ppermute | solution.py:280
  70.5 41.0 %collective-permute-start.2 = (bf16[512,896]{1,0:T(8,128)(2,1)}, bf16[512,896]{1,0:T(8,128)(2,1)}, u32[]{:S(2)}, u32[]{:S(2)}) collective-permute-start(bf16[512,896]{1,0:T(8,128)(2,1)} %multiply_convert_fusion), channel_id=1, source_target_pairs={{0,1},{1,0},{2,3},{3,2},{4,5},{5,4},{6,7},{7,6},{8,9},{9,8},{10,11... | collective-permute-start | bytes 2752520 | tf_op jit(solution)/shard_map/ppermute | solution.py:280
  78.9 35.5 %collective-permute-start.3 = (bf16[512,896]{1,0:T(8,128)(2,1)}, bf16[512,896]{1,0:T(8,128)(2,1)}, u32[]{:S(2)}, u32[]{:S(2)}) collective-permute-start(bf16[512,896]{1,0:T(8,128)(2,1)} %param.21), channel_id=1, source_target_pairs={{0,1},{1,0},{2,3},{3,2},{4,5},{5,4},{6,7},{7,6},{8,9},{9,8},{10,11... | collective-permute-start | bytes 2752520 | tf_op jit(solution)/shard_map/ppermute | solution.py:280
  90.8 56.5 %collective-permute-start.5 = (bf16[512,896]{1,0:T(8,128)(2,1)}, bf16[512,896]{1,0:T(8,128)(2,1)S(1)}, u32[]{:S(2)}, u32[]{:S(2)}) collective-permute-start(bf16[512,896]{1,0:T(8,128)(2,1)} %collective-permute-done.4), channel_id=1, source_target_pairs={{0,1},{1,0},{2,3},{3,2},{4,5},{5,4},{6,7},{7,6},{8,9},{9,8},{10,11... | collective-permute-start | bytes 2752520 | tf_op jit(solution)/shard_map/ppermute | solution.py:280
  103.7 43.8 %collective-permute-start.7 = (bf16[512,896]{1,0:T(8,128)(2,1)}, bf16[512,896]{1,0:T(8,128)(2,1)S(1)}, u32[]{:S(2)}, u32[]{:S(2)}) collective-permute-start(bf16[512,896]{1,0:T(8,128)(2,1)} %collective-permute-done.6), channel_id=1, source_target_pairs={{0,1},{1,0},{2,3},{3,2},{4,5},{5,4},{6,7},{7,6},{8,9},{9,8},{10,11... | collective-permute-start | bytes 2752520 | tf_op jit(solution)/shard_map/ppermute | solution.py:280
  143.7 123.0 %collective-permute-start.8 = (bf16[512,896]{1,0:T(8,128)(2,1)}, bf16[512,896]{1,0:T(8,128)(2,1)}, u32[]{:S(2)}, u32[]{:S(2)}) collective-permute-start(bf16[512,896]{1,0:T(8,128)(2,1)} %slice.114), channel_id=1, source_target_pairs={{0,1},{1,0},{2,3},{3,2},{4,5},{5,4},{6,7},{7,6},{8,9},{9,8},{10,11... | collective-permute-start | bytes 2752520 | tf_op jit(solution)/shard_map/ppermute | solution.py:280
  177.0 39.9 %collective-permute-start.9 = (bf16[512,896]{1,0:T(8,128)(2,1)}, bf16[512,896]{1,0:T(8,128)(2,1)}, u32[]{:S(2)}, u32[]{:S(2)}) collective-permute-start(bf16[512,896]{1,0:T(8,128)(2,1)} %slice.116), channel_id=1, source_target_pairs={{0,1},{1,0},{2,3},{3,2},{4,5},{5,4},{6,7},{7,6},{8,9},{9,8},{10,11... | collective-permute-start | bytes 2752520 | tf_op jit(solution)/shard_map/ppermute | solution.py:280
  189.7 32.0 %collective-permute-start.37 = (bf16[4,112,1216]{2,1,0:T(8,128)(2,1)}, bf16[4,112,1216]{2,1,0:T(8,128)(2,1)S(1)}, u32[]{:S(2)}, u32[]{:S(2)}) collective-permute-start(bf16[4,112,1216]{2,1,0:T(8,128)(2,1)} %dynamic-slice_bitcast_fusion.2), channel_id=1, source_target_pairs={{0,4},{4,0},{8,12},{12,8},{16,20},{20,16},{24,28},{28,24},{1,5},{5... | collective-permute-start | bytes 3268616 | tf_op jit(solution)/shard_map/ppermute | solution.py:280
  203.0 39.6 %collective-permute-start.40 = (bf16[4,112,1216]{2,1,0:T(8,128)(2,1)S(1)}, bf16[4,112,1216]{2,1,0:T(8,128)(2,1)S(1)}, u32[]{:S(2)}, u32[]{:S(2)}) collective-permute-start(bf16[4,112,1216]{2,1,0:T(8,128)(2,1)S(1)} %dynamic-slice_bitcast_fusion.1), channel_id=1, source_target_pairs={{0,4},{4,0},{8,12},{12,8},{16,20},{20,16},{24,28},{28,24},{1,5},{5... | collective-permute-start | bytes 3268616 | tf_op jit(solution)/shard_map/ppermute | solution.py:280
  214.9 51.6 %collective-permute-start.43 = (bf16[4,112,1216]{2,1,0:T(8,128)(2,1)S(1)}, bf16[4,112,1216]{2,1,0:T(8,128)(2,1)S(1)}, u32[]{:S(2)}, u32[]{:S(2)}) collective-permute-start(bf16[4,112,1216]{2,1,0:T(8,128)(2,1)S(1)} %dynamic-slice_bitcast_fusion), channel_id=1, source_target_pairs={{0,4},{4,0},{8,12},{12,8},{16,20},{20,16},{24,28},{28,24},{1,5},{5... | collective-permute-start | bytes 3268616 | tf_op jit(solution)/shard_map/ppermute | solution.py:280
  219.6 23.0 %copy-start.29 = (bf16[896,1216]{1,0:T(8,128)(2,1)S(1)}, bf16[896,1216]{1,0:T(8,128)(2,1)}, u32[]{:S(2)}) copy-start(bf16[896,1216]{1,0:T(8,128)(2,1)} %weight_grad.4) | copy-start | bytes 6537220
  219.6 47.1 %collective-permute-start.10 = (bf16[512,896]{1,0:T(8,128)(2,1)S(1)}, bf16[512,896]{1,0:T(8,128)(2,1)S(1)}, u32[]{:S(2)}, u32[]{:S(2)}) collective-permute-start(bf16[512,896]{1,0:T(8,128)(2,1)S(1)} %add_convert_fusion.2), channel_id=1, source_target_pairs={{0,2},{1,3},{2,0},{3,1},{4,6},{5,7},{6,4},{7,5},{8,10},{9,11},{10,... | collective-permute-start | bytes 2752520 | tf_op jit(solution)/shard_map/ppermute | solution.py:280
  222.0 44.5 %copy-start.28 = (bf16[896,1216]{1,0:T(8,128)(2,1)S(1)}, bf16[896,1216]{1,0:T(8,128)(2,1)}, u32[]{:S(2)}) copy-start(bf16[896,1216]{1,0:T(8,128)(2,1)} %weight_grad.5) | copy-start | bytes 6537220
  222.0 50.2 %collective-permute-start.38 = (bf16[2,112,1216]{2,1,0:T(8,128)(2,1)S(1)}, bf16[2,112,1216]{2,1,0:T(8,128)(2,1)S(1)}, u32[]{:S(2)}, u32[]{:S(2)}) collective-permute-start(bf16[2,112,1216]{2,1,0:T(8,128)(2,1)S(1)} %fusion.15), channel_id=1, source_target_pairs={{0,8},{4,12},{8,0},{12,4},{16,24},{20,28},{24,16},{28,20},{1,9},{5... | collective-permute-start | bytes 1634312 | tf_op jit(solution)/shard_map/ppermute | solution.py:280
  242.9 23.9 %copy-start.7 = (f32[512,896]{1,0:T(8,128)S(1)}, f32[512,896]{1,0:T(8,128)}, u32[]{:S(2)}) copy-start(f32[512,896]{1,0:T(8,128)} %copy-done.6) | copy-start | bytes 5505028
  242.9 23.9 %copy-start.34 = (bf16[1024,896]{1,0:T(8,128)(2,1)S(1)}, bf16[1024,896]{1,0:T(8,128)(2,1)}, u32[]{:S(2)}) copy-start(bf16[1024,896]{1,0:T(8,128)(2,1)} %get-tuple-element.34) | copy-start | bytes 5505028
  242.9 23.9 %copy-start.44 = (f32[896]{0:T(1024)S(1)}, f32[896]{0:T(1024)}, u32[]{:S(2)}) copy-start(f32[896]{0:T(1024)} %convert_element_type.332) | copy-start | bytes 10756
  242.9 23.9 %copy-start.46 = (f32[512]{0:T(512)S(1)}, f32[512]{0:T(512)}, u32[]{:S(2)}) copy-start(f32[512]{0:T(512)} %copy-done.45) | copy-start | bytes 6148
  242.9 35.2 %collective-permute-start.41 = (bf16[2,112,1216]{2,1,0:T(8,128)(2,1)S(1)}, bf16[2,112,1216]{2,1,0:T(8,128)(2,1)S(1)}, u32[]{:S(2)}, u32[]{:S(2)}) collective-permute-start(bf16[2,112,1216]{2,1,0:T(8,128)(2,1)S(1)} %fusion.16), channel_id=1, source_target_pairs={{0,8},{4,12},{8,0},{12,4},{16,24},{20,28},{24,16},{28,20},{1,9},{5... | collective-permute-start | bytes 1634312 | tf_op jit(solution)/shard_map/ppermute | solution.py:280
  269.5 6.3 %collective-permute-start.12 = (bf16[512,896]{1,0:T(8,128)(2,1)S(1)}, bf16[512,896]{1,0:T(8,128)(2,1)S(1)}, u32[]{:S(2)}, u32[]{:S(2)}) collective-permute-start(bf16[512,896]{1,0:T(8,128)(2,1)S(1)} %get-tuple-element.39), channel_id=1, source_target_pairs={{0,1},{1,0},{2,3},{3,2},{4,5},{5,4},{6,7},{7,6},{8,9},{9,8},{10,11... | collective-permute-start | bytes 2752520 | tf_op jit(solution)/shard_map/ppermute | solution.py:280
  270.4 112.3 %collective-permute-start.44 = (bf16[2,112,1216]{2,1,0:T(8,128)(2,1)}, bf16[2,112,1216]{2,1,0:T(8,128)(2,1)}, u32[]{:S(2)}, u32[]{:S(2)}) collective-permute-start(bf16[2,112,1216]{2,1,0:T(8,128)(2,1)} %fusion.17), channel_id=1, source_target_pairs={{0,8},{4,12},{8,0},{12,4},{16,24},{20,28},{24,16},{28,20},{1,9},{5... | collective-permute-start | bytes 1634312 | tf_op jit(solution)/shard_map/ppermute | solution.py:280
  273.2 128.5 %collective-permute-start.39 = (bf16[1,112,1216]{2,1,0:T(8,128)(2,1)}, bf16[1,112,1216]{2,1,0:T(8,128)(2,1)}, u32[]{:S(2)}, u32[]{:S(2)}) collective-permute-start(bf16[1,112,1216]{2,1,0:T(8,128)(2,1)} %dynamic-slice_convert_fusion.7), channel_id=1, source_target_pairs={{0,16},{4,20},{8,24},{12,28},{16,0},{20,4},{24,8},{28,12},{1,17},{... | collective-permute-start | bytes 817160 | tf_op jit(solution)/shard_map/ppermute | solution.py:280
  275.8 4.2 collective-permute-start.11
  276.0 23.1 %collective-permute-start.13 = (bf16[512,896]{1,0:T(8,128)(2,1)S(1)}, bf16[512,896]{1,0:T(8,128)(2,1)S(1)}, u32[]{:S(2)}, u32[]{:S(2)}) collective-permute-start(bf16[512,896]{1,0:T(8,128)(2,1)S(1)} %add_convert_fusion.1), channel_id=1, source_target_pairs={{0,2},{1,3},{2,0},{3,1},{4,6},{5,7},{6,4},{7,5},{8,10},{9,11},{10,... | collective-permute-start | bytes 2752520 | tf_op jit(solution)/shard_map/ppermute | solution.py:280
  279.1 181.3 %collective-permute-start.42 = (bf16[1,112,1216]{2,1,0:T(8,128)(2,1)}, bf16[1,112,1216]{2,1,0:T(8,128)(2,1)}, u32[]{:S(2)}, u32[]{:S(2)}) collective-permute-start(bf16[1,112,1216]{2,1,0:T(8,128)(2,1)} %dynamic-slice_convert_fusion.6), channel_id=1, source_target_pairs={{0,16},{4,20},{8,24},{12,28},{16,0},{20,4},{24,8},{28,12},{1,17},{... | collective-permute-start | bytes 817160 | tf_op jit(solution)/shard_map/ppermute | solution.py:280
  280.0 22.2 %copy-start.56 = (bf16[896,896]{1,0:T(8,128)(2,1)S(1)}, bf16[896,896]{1,0:T(8,128)(2,1)}, u32[]{:S(2)}) copy-start(bf16[896,896]{1,0:T(8,128)(2,1)} %param.16) | copy-start | bytes 4816900
  305.5 54.3 %copy-start.11 = (f32[896,896]{1,0:T(8,128)}, f32[896,896]{1,0:T(8,128)S(1)}, u32[]{:S(2)}) copy-start(f32[896,896]{1,0:T(8,128)S(1)} %fusion.26) | copy-start | bytes 9633796
  322.7 12.0 %copy-start.32 = (f32[896,512]{1,0:T(8,128)S(1)}, f32[896,512]{1,0:T(8,128)}, u32[]{:S(2)}) copy-start(f32[896,512]{1,0:T(8,128)} %get-tuple-element.41) | copy-start | bytes 5505028
  324.1 11.8 %collective-permute-start.15 = (bf16[256,512]{1,0:T(8,128)(2,1)S(1)}, bf16[256,512]{1,0:T(8,128)(2,1)S(1)}, u32[]{:S(2)}, u32[]{:S(2)}) collective-permute-start(bf16[256,512]{1,0:T(8,128)(2,1)S(1)} %get-tuple-element.62), channel_id=1, source_target_pairs={{0,1},{1,0},{2,3},{3,2},{4,5},{5,4},{6,7},{7,6},{8,9},{9,8},{10,11... | collective-permute-start | bytes 786440 | tf_op jit(solution)/shard_map/ppermute | solution.py:280
  334.7 26.3 %collective-permute-start.14 = (bf16[256,512]{1,0:T(8,128)(2,1)S(1)}, bf16[256,512]{1,0:T(8,128)(2,1)S(1)}, u32[]{:S(2)}, u32[]{:S(2)}) collective-permute-start(bf16[256,512]{1,0:T(8,128)(2,1)S(1)} %get-tuple-element.61), channel_id=1, source_target_pairs={{0,1},{1,0},{2,3},{3,2},{4,5},{5,4},{6,7},{7,6},{8,9},{9,8},{10,11... | collective-permute-start | bytes 786440 | tf_op jit(solution)/shard_map/ppermute | solution.py:280
  336.6 30.1 %collective-permute-start.16 = (bf16[256,512]{1,0:T(8,128)(2,1)S(1)}, bf16[256,512]{1,0:T(8,128)(2,1)S(1)}, u32[]{:S(2)}, u32[]{:S(2)}) collective-permute-start(bf16[256,512]{1,0:T(8,128)(2,1)S(1)} %add_convert_fusion.7), channel_id=1, source_target_pairs={{0,2},{1,3},{2,0},{3,1},{4,6},{5,7},{6,4},{7,5},{8,10},{9,11},{10,... | collective-permute-start | bytes 786440 | tf_op jit(solution)/shard_map/ppermute | solution.py:280
  360.9 17.8 %collective-permute-start.27 = (bf16[2,224,896]{2,1,0:T(8,128)(2,1)}, bf16[2,224,896]{2,1,0:T(8,128)(2,1)}, u32[]{:S(2)}, u32[]{:S(2)}) collective-permute-start(bf16[2,224,896]{2,1,0:T(8,128)(2,1)} %fusion.14), channel_id=1, source_target_pairs={{0,1},{1,0},{2,3},{3,2},{4,5},{5,4},{6,7},{7,6},{8,9},{9,8},{10,11... | collective-permute-start | bytes 2408456 | tf_op jit(solution)/shard_map/ppermute | solution.py:280
  378.7 19.1 %collective-permute-start.17 = (bf16[2,224,1280]{2,1,0:T(8,128)(2,1)}, bf16[2,224,1280]{2,1,0:T(8,128)(2,1)}, u32[]{:S(2)}, u32[]{:S(2)}) collective-permute-start(bf16[2,224,1280]{2,1,0:T(8,128)(2,1)} %fusion.13), channel_id=1, source_target_pairs={{0,1},{1,0},{2,3},{3,2},{4,5},{5,4},{6,7},{7,6},{8,9},{9,8},{10,11... | collective-permute-start | bytes 3440648 | tf_op jit(solution)/shard_map/ppermute | solution.py:280
  380.9 11.8 %collective-permute-start.28 = (bf16[1,224,896]{2,1,0:T(8,128)(2,1)S(1)}, bf16[1,224,896]{2,1,0:T(8,128)(2,1)S(1)}, u32[]{:S(2)}, u32[]{:S(2)}) collective-permute-start(bf16[1,224,896]{2,1,0:T(8,128)(2,1)S(1)} %dynamic-slice_convert_fusion.4), channel_id=1, source_target_pairs={{0,2},{1,3},{2,0},{3,1},{4,6},{5,7},{6,4},{7,5},{8,10},{9,11},{10,... | collective-permute-start | bytes 1204232 | tf_op jit(solution)/shard_map/ppermute | solution.py:280
  383.9 16.2 %copy-start.23 = (f32[2,112,1216]{2,1,0:T(8,128)}, f32[2,112,1216]{2,1,0:T(8,128)S(1)}, u32[]{:S(2)}) copy-start(f32[2,112,1216]{2,1,0:T(8,128)S(1)} %bitcast_add_fusion.2) | copy-start | bytes 3268612
  384.7 88.9 %collective-permute-start.45 = (bf16[1,112,1216]{2,1,0:T(8,128)(2,1)}, bf16[1,112,1216]{2,1,0:T(8,128)(2,1)}, u32[]{:S(2)}, u32[]{:S(2)}) collective-permute-start(bf16[1,112,1216]{2,1,0:T(8,128)(2,1)} %dynamic-slice_convert_fusion.5), channel_id=1, source_target_pairs={{0,16},{4,20},{8,24},{12,28},{16,0},{20,4},{24,8},{28,12},{1,17},{... | collective-permute-start | bytes 817160 | tf_op jit(solution)/shard_map/ppermute | solution.py:280
  396.2 7.4 %collective-permute-start.29 = (bf16[4,28,896]{2,1,0:T(8,128)(2,1)S(1)}, bf16[4,28,896]{2,1,0:T(8,128)(2,1)S(1)}, u32[]{:S(2)}, u32[]{:S(2)}) collective-permute-start(bf16[4,28,896]{2,1,0:T(8,128)(2,1)S(1)} %dynamic-slice_bitcast_fusion.4), channel_id=1, source_target_pairs={{0,4},{4,0},{8,12},{12,8},{16,20},{20,16},{24,28},{28,24},{1,5},{5... | collective-permute-start | bytes 602120 | tf_op jit(solution)/shard_map/ppermute | solution.py:280
  400.1 14.5 %collective-permute-start.18 = (bf16[1,224,1280]{2,1,0:T(8,128)(2,1)S(1)}, bf16[1,224,1280]{2,1,0:T(8,128)(2,1)S(1)}, u32[]{:S(2)}, u32[]{:S(2)}) collective-permute-start(bf16[1,224,1280]{2,1,0:T(8,128)(2,1)S(1)} %dynamic-slice_convert_fusion.3), channel_id=1, source_target_pairs={{0,2},{1,3},{2,0},{3,1},{4,6},{5,7},{6,4},{7,5},{8,10},{9,11},{10,... | collective-permute-start | bytes 1720328 | tf_op jit(solution)/shard_map/ppermute | solution.py:280
  403.7 10.9 %copy-start.39 = (f32[4,28,896]{2,1,0:T(8,128)}, f32[4,28,896]{2,1,0:T(8,128)S(1)}, u32[]{:S(2)}) copy-start(f32[4,28,896]{2,1,0:T(8,128)S(1)} %convert_add_fusion.7) | copy-start | bytes 1204228
  403.7 11.8 %collective-permute-start.30 = (bf16[2,28,896]{2,1,0:T(8,128)(2,1)S(1)}, bf16[2,28,896]{2,1,0:T(8,128)(2,1)S(1)}, u32[]{:S(2)}, u32[]{:S(2)}) collective-permute-start(bf16[2,28,896]{2,1,0:T(8,128)(2,1)S(1)} %fusion.33), channel_id=1, source_target_pairs={{0,8},{4,12},{8,0},{12,4},{16,24},{20,28},{24,16},{28,20},{1,9},{5... | collective-permute-start | bytes 301064 | tf_op jit(solution)/shard_map/ppermute | solution.py:280
  414.9 8.3 %collective-permute-start.19 = (bf16[4,28,1280]{2,1,0:T(8,128)(2,1)S(1)}, bf16[4,28,1280]{2,1,0:T(8,128)(2,1)S(1)}, u32[]{:S(2)}, u32[]{:S(2)}) collective-permute-start(bf16[4,28,1280]{2,1,0:T(8,128)(2,1)S(1)} %dynamic-slice_bitcast_fusion.3), channel_id=1, source_target_pairs={{0,4},{4,0},{8,12},{12,8},{16,20},{20,16},{24,28},{28,24},{1,5},{5... | collective-permute-start | bytes 860168 | tf_op jit(solution)/shard_map/ppermute | solution.py:280
  416.5 7.3 %collective-permute-start.31 = (bf16[1,28,896]{2,1,0:T(8,128)(2,1)S(1)}, bf16[1,28,896]{2,1,0:T(8,128)(2,1)S(1)}, u32[]{:S(2)}, u32[]{:S(2)}) collective-permute-start(bf16[1,28,896]{2,1,0:T(8,128)(2,1)S(1)} %dynamic-slice_convert_fusion.11), channel_id=1, source_target_pairs={{0,16},{4,20},{8,24},{12,28},{16,0},{20,4},{24,8},{28,12},{1,17},{... | collective-permute-start | bytes 150536 | tf_op jit(solution)/shard_map/ppermute | solution.py:280
  423.3 5.9 %collective-permute-start.20 = (bf16[2,28,1280]{2,1,0:T(8,128)(2,1)S(1)}, bf16[2,28,1280]{2,1,0:T(8,128)(2,1)S(1)}, u32[]{:S(2)}, u32[]{:S(2)}) collective-permute-start(bf16[2,28,1280]{2,1,0:T(8,128)(2,1)S(1)} %fusion.32), channel_id=1, source_target_pairs={{0,8},{4,12},{8,0},{12,4},{16,24},{20,28},{24,16},{28,20},{1,9},{5... | collective-permute-start | bytes 430088 | tf_op jit(solution)/shard_map/ppermute | solution.py:280
  423.8 6.8 %collective-permute-start.32 = (bf16[1,28,896]{2,1,0:T(8,128)(2,1)S(1)}, bf16[1,28,896]{2,1,0:T(8,128)(2,1)S(1)}, u32[]{:S(2)}, u32[]{:S(2)}) collective-permute-start(bf16[1,28,896]{2,1,0:T(8,128)(2,1)S(1)} %add_convert_fusion.10), channel_id=1, source_target_pairs={{0,16},{4,20},{8,24},{12,28},{16,0},{20,4},{24,8},{28,12},{1,17},{... | collective-permute-start | bytes 150536 | tf_op jit(solution)/shard_map/ppermute | solution.py:280
  429.2 7.7 %collective-permute-start.21 = (bf16[1,28,1280]{2,1,0:T(8,128)(2,1)S(1)}, bf16[1,28,1280]{2,1,0:T(8,128)(2,1)S(1)}, u32[]{:S(2)}, u32[]{:S(2)}) collective-permute-start(bf16[1,28,1280]{2,1,0:T(8,128)(2,1)S(1)} %dynamic-slice_convert_fusion.10), channel_id=1, source_target_pairs={{0,16},{4,20},{8,24},{12,28},{16,0},{20,4},{24,8},{28,12},{1,17},{... | collective-permute-start | bytes 215048 | tf_op jit(solution)/shard_map/ppermute | solution.py:280
  436.9 5.5 %collective-permute-start.22 = (bf16[1,28,1280]{2,1,0:T(8,128)(2,1)S(1)}, bf16[1,28,1280]{2,1,0:T(8,128)(2,1)S(1)}, u32[]{:S(2)}, u32[]{:S(2)}) collective-permute-start(bf16[1,28,1280]{2,1,0:T(8,128)(2,1)S(1)} %add_convert_fusion.8), channel_id=1, source_target_pairs={{0,16},{4,20},{8,24},{12,28},{16,0},{20,4},{24,8},{28,12},{1,17},{... | collective-permute-start | bytes 215048 | tf_op jit(solution)/shard_map/ppermute | solution.py:280
  437.0 6.5 %collective-permute-start.33 = (bf16[2,28,896]{2,1,0:T(8,128)(2,1)S(1)}, bf16[2,28,896]{2,1,0:T(8,128)(2,1)S(1)}, u32[]{:S(2)}, u32[]{:S(2)}) collective-permute-start(bf16[2,28,896]{2,1,0:T(8,128)(2,1)S(1)} %maximum_bitcast_fusion.3), channel_id=1, source_target_pairs={{0,8},{4,12},{8,0},{12,4},{16,24},{20,28},{24,16},{28,20},{1,9},{5... | collective-permute-start | bytes 301064 | tf_op jit(solution)/shard_map/ppermute | solution.py:280
  442.5 5.4 %collective-permute-start.23 = (bf16[2,28,1280]{2,1,0:T(8,128)(2,1)S(1)}, bf16[2,28,1280]{2,1,0:T(8,128)(2,1)S(1)}, u32[]{:S(2)}, u32[]{:S(2)}) collective-permute-start(bf16[2,28,1280]{2,1,0:T(8,128)(2,1)S(1)} %maximum_bitcast_fusion.2), channel_id=1, source_target_pairs={{0,8},{4,12},{8,0},{12,4},{16,24},{20,28},{24,16},{28,20},{1,9},{5... | collective-permute-start | bytes 430088 | tf_op jit(solution)/shard_map/ppermute | solution.py:280
  443.6 8.3 %collective-permute-start.34 = (bf16[4,28,896]{2,1,0:T(8,128)(2,1)S(1)}, bf16[4,28,896]{2,1,0:T(8,128)(2,1)S(1)}, u32[]{:S(2)}, u32[]{:S(2)}) collective-permute-start(bf16[4,28,896]{2,1,0:T(8,128)(2,1)S(1)} %bitcast.280), channel_id=1, source_target_pairs={{0,4},{4,0},{8,12},{12,8},{16,20},{20,16},{24,28},{28,24},{1,5},{5... | collective-permute-start | bytes 602120 | tf_op jit(solution)/shard_map/ppermute | solution.py:280
  448.0 7.6 %collective-permute-start.24 = (bf16[4,28,1280]{2,1,0:T(8,128)(2,1)S(1)}, bf16[4,28,1280]{2,1,0:T(8,128)(2,1)}, u32[]{:S(2)}, u32[]{:S(2)}) collective-permute-start(bf16[4,28,1280]{2,1,0:T(8,128)(2,1)S(1)} %bitcast.275), channel_id=1, source_target_pairs={{0,4},{4,0},{8,12},{12,8},{16,20},{20,16},{24,28},{28,24},{1,5},{5... | collective-permute-start | bytes 860168 | tf_op jit(solution)/shard_map/ppermute | solution.py:280
  452.9 7.5 %copy-start.22 = (f32[2,112,1216]{2,1,0:T(8,128)S(1)}, f32[2,112,1216]{2,1,0:T(8,128)}, u32[]{:S(2)}) copy-start(f32[2,112,1216]{2,1,0:T(8,128)} %copy-done.21) | copy-start | bytes 3268612
  452.9 10.5 %collective-permute-start.35 = (bf16[1,224,896]{2,1,0:T(8,128)(2,1)}, bf16[1,224,896]{2,1,0:T(8,128)(2,1)}, u32[]{:S(2)}, u32[]{:S(2)}) collective-permute-start(bf16[1,224,896]{2,1,0:T(8,128)(2,1)} %reshape_reshape.34), channel_id=1, source_target_pairs={{0,2},{1,3},{2,0},{3,1},{4,6},{5,7},{6,4},{7,5},{8,10},{9,11},{10,... | collective-permute-start | bytes 1204232 | tf_op jit(solution)/shard_map/ppermute | solution.py:280
  459.6 13.7 %collective-permute-start.25 = (bf16[1,224,1280]{2,1,0:T(8,128)(2,1)}, bf16[1,224,1280]{2,1,0:T(8,128)(2,1)S(1)}, u32[]{:S(2)}, u32[]{:S(2)}) collective-permute-start(bf16[1,224,1280]{2,1,0:T(8,128)(2,1)} %reshape_reshape.31), channel_id=1, source_target_pairs={{0,2},{1,3},{2,0},{3,1},{4,6},{5,7},{6,4},{7,5},{8,10},{9,11},{10,... | collective-permute-start | bytes 1720328 | tf_op jit(solution)/shard_map/ppermute | solution.py:280
  462.3 11.0 %copy-start.31 = (bf16[1,224,1280]{2,1,0:T(8,128)(2,1)S(1)}, bf16[1,224,1280]{2,1,0:T(8,128)(2,1)}, u32[]{:S(2)}) copy-start(bf16[1,224,1280]{2,1,0:T(8,128)(2,1)} %reshape_reshape.31) | copy-start | bytes 1720324
  464.7 8.9 %copy-start.24 = (f32[2,112,1216]{2,1,0:T(8,128)S(1)}, f32[2,112,1216]{2,1,0:T(8,128)}, u32[]{:S(2)}) copy-start(f32[2,112,1216]{2,1,0:T(8,128)} %copy-done.23) | copy-start | bytes 3268612
  464.7 12.8 %collective-permute-start.36 = (bf16[2,224,896]{2,1,0:T(8,128)(2,1)S(1)}, bf16[2,224,896]{2,1,0:T(8,128)(2,1)S(1)}, u32[]{:S(2)}, u32[]{:S(2)}) collective-permute-start(bf16[2,224,896]{2,1,0:T(8,128)(2,1)S(1)} %maximum_bitcast_fusion.1), channel_id=1, source_target_pairs={{0,1},{1,0},{2,3},{3,2},{4,5},{5,4},{6,7},{7,6},{8,9},{9,8},{10,11... | collective-permute-start | bytes 2408456 | tf_op jit(solution)/shard_map/ppermute | solution.py:280
  473.5 6.3 %collective-permute-start.26 = (bf16[2,224,1280]{2,1,0:T(8,128)(2,1)S(1)}, bf16[2,224,1280]{2,1,0:T(8,128)(2,1)S(1)}, u32[]{:S(2)}, u32[]{:S(2)}) collective-permute-start(bf16[2,224,1280]{2,1,0:T(8,128)(2,1)S(1)} %maximum_bitcast_fusion), channel_id=1, source_target_pairs={{0,1},{1,0},{2,3},{3,2},{4,5},{5,4},{6,7},{7,6},{8,9},{9,8},{10,11... | collective-permute-start | bytes 3440648 | tf_op jit(solution)/shard_map/ppermute | solution.py:280
  (40 other events, 118.2 us)
